TPU v7x, 32 devices: a whole 2x2x4 slice. The times are simulated.
32 devices in a mesh: mode: 2 (over x), sx: 4 (over z), sy: 4 (over y, core).
Axes of the slice: x: 2, y: 2, z: 4, core: 2. Of those that a mesh axis runs over, the one named last changes fastest.
Arguments:
- start_field: float32 [2048, 16, 512], P('mode', 'sx', 'sy'), may hold values from -2.5 to 2.5
- right_side: float32 [2048, 16, 512], P('mode', 'sx', 'sy'), may hold values from -6 to 6
- mean_coef: float32 [16, 512], P('sx', 'sy'), may hold values from 0.5 to 2
- term_coef: float32 [8, 16, 512], P(None, 'sx', 'sy'), may hold values from -3 to 3
- coupling: float32 [8, 2048, 2048], P(None, None, 'mode'), may hold values from -0.05 to 0.05, as said below
- block_mask: int32 [8, 16, 16], replicated, may hold values from 0 to 1, as said below
Outputs:
- solution: float32 [2048, 16, 512], P('mode', 'sx', 'sy')
- residual: float32 [2048, 16, 512], P('mode', 'sx', 'sy')
Inputs may be any that keep to these rules, and one draw needn't show every extreme that they name: coupling[t] is symmetric: coupling[t, i, j] = coupling[t, j, i]. block_mask[t] is symmetric; entry [t, a, b] covers modes a * 128 to (a + 1) * 128 - 1 against b * 128 to (b + 1) * 128 - 1.
All inputs are finite; a program needn't handle non-finite values.
Results may differ from a plain program's by a relative error of at most 0.0002.
Values sent between devices are 32-bit elements; how exact they have to be, the bound alone decides.
No kernel may reach another device: no remote copies, remote signals or barrier semaphores. Data moves between devices by JAX's collectives and lax.ppermute only.
A program may use at most 256 MiB of HBM per device.

v0:
```python
import functools

import jax
import jax.numpy as jnp
from jax import lax
from jax.experimental import pallas as pl
from jax.experimental.pallas import tpu as pltpu
from jax.sharding import PartitionSpec as P

SWEEPS = 3

react = 0.5
theta = 8.5
delta = 8.0

LANES = 128
GROUP = 8
PAIR = 2
SLOTS = 3
CHUNKS = 2
PAD = 16
SUB = 32
UNROLL = 4
VMEM_LIMIT = 24 * 1024 * 1024

f32 = jnp.float32
bf16 = jnp.bfloat16


def params():
    return pltpu.CompilerParams(vmem_limit_bytes=VMEM_LIMIT)


def whole():
    return pl.BlockSpec(memory_space=pltpu.VMEM)


def smem():
    return pl.BlockSpec(memory_space=pltpu.SMEM)


def cubic():
    def add(a, b):
        size = max(len(a), len(b))
        a = a + [0.0] * (size - len(a))
        b = b + [0.0] * (size - len(b))
        return [x + y for x, y in zip(a, b)]

    def scale(a, s):
        return [x * s for x in a]

    def apply(a):
        return add(scale(a, theta), [0.0] + scale(a, delta))

    sigma = theta / delta
    rho = 1.0 / sigma
    total = [0.0]
    step = [1.0 / theta]
    for k in range(SWEEPS + 1):
        total = add(total, step)
        if k < SWEEPS:
            misfit = add([1.0], scale(apply(total), -1.0))
            rho_next = 1.0 / (2.0 * sigma - rho)
            step = add(scale(step, rho_next * rho), scale(misfit, 2.0 * rho_next / delta))
            rho = rho_next
    return total


def lane_iota(shape):
    return lax.broadcasted_iota(jnp.int32, shape, 1)


def row_iota(shape):
    return lax.broadcasted_iota(jnp.int32, shape, 0)


def pack_kernel(modes, terms, f_ref, mean_ref, term_ref, up_ref, down_ref, left_ref, right_ref):
    up_ref[0:modes, :] = f_ref[pl.ds(3, modes, stride=4), :]
    down_ref[0:modes, :] = f_ref[pl.ds(0, modes, stride=4), :]
    for ref, x in ((up_ref, 3), (down_ref, 0)):
        ref[modes : modes + terms, :] = term_ref[pl.ds(x, terms, stride=4), :]
        ref[modes + terms : modes + terms + 1, :] = mean_ref[x : x + 1, :]
        ref[modes + terms + 1 : modes + PAD, :] = jnp.zeros((PAD - terms - 1, LANES), f32)
    shape = (LANES, LANES)
    lane = lane_iota(shape)
    for m in range(modes // LANES):
        tile = jnp.zeros(shape, f32)
        for x in range(4):
            v = f_ref[pl.ds(m * 4 * LANES + x, LANES, stride=4), :]
            tile = jnp.where(lane == x, pltpu.roll(v, x, 1) if x else v, tile)
            tile = jnp.where(lane == 8 + x, pltpu.roll(v, 9 + x, 1), tile)
        turned = tile.T
        left_ref[:, m * LANES : (m + 1) * LANES] = turned[0:8, :]
        right_ref[:, m * LANES : (m + 1) * LANES] = turned[8:16, :]
    rows = terms * 4
    coefs = jnp.concatenate([term_ref[...], mean_ref[...], jnp.zeros((LANES - rows - 4, LANES), f32)], axis=0)
    turned = coefs.T
    for k in range(SWEEPS):
        left_ref[4 + k : 5 + k, 0:LANES] = turned[k : k + 1, :]
        right_ref[4 + k : 5 + k, 0:LANES] = turned[LANES - 1 - k : LANES - k, :]


def list_sizes(terms, blocks, part):
    most = -(-terms * blocks // GROUP)
    groups = part * most + PAIR
    return groups * GROUP + GROUP, groups + most


def list_kernel(segments, terms, blocks, part, mask_ref, list_ref, row_ref, count_ref):
    length, rows = list_sizes(terms, blocks, part)
    most = -(-terms * blocks // GROUP)
    none = terms * blocks
    me = lax.axis_index("mode")

    def per_segment(o, _):
        def per_row(a, base):
            count = base
            for t in range(terms):
                found = [mask_ref[t, o * part + a, me * blocks + b] for b in range(blocks)]
                for b in range(blocks):
                    list_ref[o * length + count] = t * blocks + b
                    count = count + found[b]
            for k in range(GROUP):
                list_ref[o * length + count + k] = none
            group = base // GROUP
            for k in range(most):
                row_ref[o * rows + group + k] = a
            return base + (count - base + GROUP - 1) // GROUP * GROUP

        total = lax.fori_loop(0, part, per_row, 0)
        for k in range((PAIR - 1) * GROUP):
            list_ref[o * length + total + k] = none
        for k in range(PAIR - 1):
            row_ref[o * rows + total // GROUP + k] = 0
        count_ref[o] = (total // GROUP + PAIR - 1) // PAIR
        return 0

    lax.fori_loop(0, segments, per_segment, 0)


def flux_kernel(cfg, *refs):
    modes, terms, rows, edge = cfg
    refs = list(refs)
    f_ref = refs.pop(0)
    if edge:
        low_ref, high_ref = refs[:2]
        refs = refs[2:]
    left_ref, right_ref, mean_ref, term_ref, rs_ref, fh_ref, fl_ref, out_ref, w_ref, h_ref, hc_ref = refs

    square = (LANES, LANES)
    srow = row_iota(square)
    corner = jnp.where(
        srow == 0,
        left_ref[4:5, 0:LANES],
        jnp.where(srow == LANES - 1, right_ref[4:5, 0:LANES], 0.0),
    )
    hc_ref[...] = corner.T

    def coefs(x):
        if x < 0:
            return low_ref[modes : modes + terms, :], low_ref[modes + terms : modes + terms + 1, :]
        if x > 3:
            return high_ref[modes : modes + terms, :], high_ref[modes + terms : modes + terms + 1, :]
        return term_ref[pl.ds(x, terms, stride=4), :], mean_ref[x : x + 1, :]

    for i, x in enumerate(rows):
        center = coefs(x)
        before = coefs(x - 1)
        after = coefs(x + 1)
        side = (hc_ref[pl.ds(x, terms, stride=4), :], hc_ref[terms * 4 + x : terms * 4 + x + 1, :])
        for j, (lo, size) in enumerate(((0, terms), (terms, 1))):
            c = center[j]
            lane = lane_iota(c.shape)
            to_left = jnp.where(lane == 0, side[j], pltpu.roll(c, 1, 1))
            to_right = jnp.where(lane == LANES - 1, side[j], pltpu.roll(c, LANES - 1, 1))
            for k, other in enumerate((before[j], after[j], to_left, to_right)):
                w_ref[i, k, lo : lo + size, :] = 0.5 * (c + other)

    x0, x1 = rows
    half = LANES // 2
    for m in range(modes // LANES):
        cols = slice(m * LANES, (m + 1) * LANES)
        q = jnp.zeros(square, f32)
        for at, ref, x in (
            (0, left_ref, x0),
            (LANES - 1, right_ref, x0),
            (half, left_ref, x1),
            (half - 1, right_ref, x1),
        ):
            q = jnp.where(srow == at, ref[x : x + 1, cols], q)
        turned = q.T
        h_ref[0, cols, :] = turned
        h_ref[1, cols, :] = pltpu.roll(turned, half, 1)

    sub = 32

    def fluxes(s, _):
        m = pl.multiple_of(s * sub, sub)
        lane = lane_iota((sub, LANES))

        def value(x):
            if x < 0:
                return low_ref[pl.ds(m, sub), :]
            if x > 3:
                return high_ref[pl.ds(m, sub), :]
            return f_ref[pl.ds(m * 4 + x, sub, stride=4), :]

        for i, x in enumerate(rows):
            v = value(x)
            h = h_ref[i, pl.ds(m, sub), :]
            diffs = (
                v - value(x - 1),
                v - value(x + 1),
                v - jnp.where(lane == 0, h, pltpu.roll(v, 1, 1)),
                v - jnp.where(lane == LANES - 1, h, pltpu.roll(v, LANES - 1, 1)),
            )

            def flux(t):
                total = w_ref[i, 0, t : t + 1, :] * diffs[0]
                for k in range(1, 4):
                    total = total + w_ref[i, k, t : t + 1, :] * diffs[k]
                return total

            for t in range(terms):
                value_t = flux(t)
                high = value_t.astype(bf16)
                at = pl.multiple_of(t * modes + m, sub)
                fh_ref[pl.ds(at, sub), i * LANES : (i + 1) * LANES] = high
                fl_ref[pl.ds(at, sub), i * LANES : (i + 1) * LANES] = (value_t - high.astype(f32)).astype(bf16)
            rs = rs_ref[pl.ds(m * 4 + x, sub, stride=4), :]
            out_ref[i, pl.ds(m, sub), :] = rs - (flux(terms) + react * v)
        return 0

    lax.fori_loop(0, modes // sub, fluxes, 0)
    fh_ref[terms * modes :, :] = jnp.zeros((LANES, 2 * LANES), bf16)
    fl_ref[terms * modes :, :] = jnp.zeros((LANES, 2 * LANES), bf16)


def couple_kernel(cfg, *refs):
    terms, blocks, owners, chunks, part, shift, chunk, own = cfg
    refs = list(refs)
    list_ref, row_ref, count_ref, a_ref, fh_ref, fl_ref = refs[:6]
    refs = refs[6:]
    if own:
        base_ref = refs.pop(0)
    out_ref, slot_ref, sem = refs
    length, row_len = list_sizes(terms, blocks, part)
    owner = lax.rem(lax.axis_index("mode") + shift, owners)
    segment = owner * chunks + chunk
    steps = count_ref[segment]
    none = terms * blocks
    step_blocks = PAIR * GROUP

    def fetch(step, slot):
        for p in range(PAIR):
            a = row_ref[segment * row_len + step * PAIR + p]
            row = pl.multiple_of(((owner * chunks + chunk) * part + a) * LANES, LANES)
            for k in range(p * GROUP, (p + 1) * GROUP):
                e = jnp.minimum(list_ref[segment * length + step * step_blocks + k], none - 1)
                t = e // blocks
                b = e - t * blocks
                pltpu.make_async_copy(
                    a_ref.at[t, pl.ds(row, LANES), pl.ds(pl.multiple_of(b * LANES, LANES), LANES)],
                    slot_ref.at[slot, k],
                    sem.at[slot],
                ).start()

    for i in range(SLOTS - 1):
        @pl.when(i < steps)
        def _():
            fetch(i, i)

    if own:
        out_ref[...] = base_ref[:, chunk * part * LANES : (chunk + 1) * part * LANES, :]
    else:
        out_ref[...] = jnp.zeros(out_ref.shape, f32)

    def product(step, _):
        slot = lax.rem(step, SLOTS)

        @pl.when(step + SLOTS - 1 < steps)
        def _():
            fetch(step + SLOTS - 1, lax.rem(step + SLOTS - 1, SLOTS))

        pltpu.make_async_copy(slot_ref.at[slot], slot_ref.at[slot], sem.at[slot]).wait()
        for p in range(PAIR):
            highs, lows, fhs, fls = [], [], [], []
            for k in range(p * GROUP, (p + 1) * GROUP):
                block = slot_ref[slot, k]
                high = block.astype(bf16)
                highs.append(high)
                lows.append((block - high.astype(f32)).astype(bf16))
                at = pl.multiple_of(list_ref[segment * length + step * step_blocks + k] * LANES, LANES)
                fhs.append(fh_ref[pl.ds(at, LANES), :])
                fls.append(fl_ref[pl.ds(at, LANES), :])
            high = jnp.concatenate(highs, axis=1)
            low = jnp.concatenate(lows, axis=1)
            fh = jnp.concatenate(fhs, axis=0)
            fl = jnp.concatenate(fls, axis=0)
            both = jnp.dot(jnp.concatenate([high, low], axis=0), fh, preferred_element_type=f32)
            total = both[:LANES] + both[LANES:] + jnp.dot(high, fl, preferred_element_type=f32)
            to = pl.ds(pl.multiple_of(row_ref[segment * row_len + step * PAIR + p] * LANES, LANES), LANES)
            for i in range(2):
                piece = total[:, i * LANES : (i + 1) * LANES]
                if own:
                    out_ref[i, to, :] = out_ref[i, to, :] - piece
                else:
                    out_ref[i, to, :] = out_ref[i, to, :] + piece
        return 0

    lax.fori_loop(0, steps, product, 0)


def finish_kernel(parts, inner_ref, base_ref, *refs):
    part_refs = refs[:parts]
    up_ref, down_ref, res_ref, side_ref = refs[-4:]
    low = base_ref[0]
    high = base_ref[1]
    for ref in part_refs:
        low = low - ref[0]
        high = high - ref[1]
    rows = (low, inner_ref[0], inner_ref[1], high)
    down_ref[...] = low
    up_ref[...] = high
    square = (LANES, LANES)
    lane = lane_iota(square)
    tile = jnp.zeros(square, f32)
    for x, v in enumerate(rows):
        res_ref[pl.ds(x, LANES, stride=4), :] = v
        moved = pltpu.roll(v, 8 * x + 3, 1)
        tile = jnp.where((lane >= 8 * x) & (lane < 8 * x + 6), moved, tile)
    side_ref[...] = tile.T[0:32, :]


def extra_kernel(tiles, side_ref, left_ref, right_ref, up_in, down_in, up_ref, down_ref):
    for ref, near, far in ((up_ref, 24, 16), (down_ref, 0, 8)):
        for k in range(tiles):
            cols = slice(k * LANES, (k + 1) * LANES)
            picks = (
                left_ref[near + 1 : near + 2, cols],
                left_ref[near + 2 : near + 3, cols],
                side_ref[near + 3 : near + 4, cols],
                side_ref[near + 2 : near + 3, cols],
                right_ref[near + 3 : near + 4, cols],
                right_ref[near + 4 : near + 5, cols],
                left_ref[far + 2 : far + 3, cols],
                right_ref[far + 3 : far + 4, cols],
            )
            for j, pick in enumerate(picks):
                ref[k * 8 + j : k * 8 + j + 1, :] = pick


COLS = (-3, -2, -1, 0, 1, 126, 127, 128, 129, 130)


def side_columns(modes, side_ref, left_ref, right_ref, low_ref, high_ref, we_ref, e_ref, q_ref, h_ref):
    beta = cubic()
    e_ref[...] = jnp.zeros(e_ref.shape, f32)
    sources = (
        (left_ref, 0), (left_ref, 1), (left_ref, 2), (side_ref, 3), (side_ref, 4),
        (side_ref, 1), (side_ref, 2), (right_ref, 3), (right_ref, 4), (right_ref, 5),
    )
    for c, (ref, k) in enumerate(sources):
        for x in range(4):
            e_ref[c, 3 + x : 4 + x, :] = ref[8 * x + k : 8 * x + k + 1, :]
    for ref, near, far in ((low_ref, 2, 1), (high_ref, 7, 8)):
        for t in range(modes // LANES):
            cols = slice(t * LANES, (t + 1) * LANES)
            for j, c in enumerate((1, 2, 3, 6, 7, 8)):
                e_ref[c, near : near + 1, cols] = ref[t * 8 + j : t * 8 + j + 1, :]
            e_ref[2, far : far + 1, cols] = ref[t * 8 + 6 : t * 8 + 7, :]
            e_ref[7, far : far + 1, cols] = ref[t * 8 + 7 : t * 8 + 8, :]

    def side_apply(values, c, j):
        v = values[c]
        w = [we_ref[:, kind * 6 + j : kind * 6 + j + 1] for kind in range(5)]
        near = w[1] * pltpu.roll(v, 1, 0) + w[2] * pltpu.roll(v, 15, 0)
        return w[0] * v - (near + w[3] * values[c - 1] + w[4] * values[c + 1])

    zero = {c: e_ref[c] for c in range(10)}
    one = {}
    for j, c in enumerate((1, 2, 3, 6, 7, 8)):
        one[c] = beta[2] * zero[c] + beta[3] * side_apply(zero, c, j)
    two = {}
    for j, c in ((1, 2), (4, 7)):
        two[c] = beta[1] * zero[c] + side_apply(one, c, j)
    q_ref[...] = jnp.zeros(q_ref.shape, f32)
    base = 0
    for values, first, size in ((zero, 1, 8), (one, 2, 6), (two, 3, 4)):
        for k in range(size):
            q_ref[base + 2 * k : base + 2 * k + 1, :] = values[7][first + k : first + k + 1]
            q_ref[base + 2 * k + 1 : base + 2 * k + 2, :] = values[2][first + k : first + k + 1]
        base += 2 * size
    for t in range(modes // LANES):
        cols = slice(t * LANES, (t + 1) * LANES)
        h_ref[cols, :] = q_ref[:, cols].T


def correct_kernel(
    modes, f_ref, inner_ref, low_in_ref, high_in_ref, up_ref, down_ref, low_ref, high_ref, low_x_ref, high_x_ref,
    side_ref, left_ref, right_ref, w_ref, we_ref, *refs,
):
    sol_ref, e_ref, q_ref, h_ref = refs[-4:]
    beta = cubic()

    @pl.when(pl.program_id(0) == 0)
    def _():
        side_columns(modes, side_ref, left_ref, right_ref, low_x_ref, high_x_ref, we_ref, e_ref, q_ref, h_ref)

    sub = SUB
    start = pl.program_id(0) * LANES

    def body(s, _):
        m = pl.multiple_of(s * sub, sub)
        at = pl.ds(m, sub)
        lane = lane_iota((sub, LANES))
        turned = h_ref[pl.ds(pl.multiple_of(start + m, sub), sub), :]
        r = {
            -3: low_in_ref[0, at, :], -2: low_in_ref[1, at, :], -1: low_ref[at, :],
            0: down_ref[at, :], 1: inner_ref[0, at, :], 2: inner_ref[1, at, :], 3: up_ref[at, :],
            4: high_ref[at, :], 5: high_in_ref[0, at, :], 6: high_in_ref[1, at, :],
        }

        def apply(values, x, p):
            v = values[x]
            h = pltpu.roll(turned, (LANES - 2 * p - 1) % LANES, 1)
            to_left = jnp.where(lane == 0, h, pltpu.roll(v, 1, 1))
            to_right = jnp.where(lane == LANES - 1, h, pltpu.roll(v, LANES - 1, 1))
            w = [w_ref[kind, x + 2 : x + 3, :] for kind in range(5)]
            near = w[1] * values[x - 1] + w[2] * values[x + 1] + w[3] * to_left + w[4] * to_right
            return w[0] * v - near

        p = 0
        first = {}
        for x in range(-2, 6):
            first[x] = beta[2] * r[x] + beta[3] * apply(r, x, p)
            p += 1
        second = {}
        for x in range(-1, 5):
            second[x] = beta[1] * r[x] + apply(first, x, p)
            p += 1
        for x in range(4):
            total = beta[0] * r[x] + apply(second, x, p)
            p += 1
            where = pl.ds(m * 4 + x, sub, stride=4)
            sol_ref[where, :] = f_ref[where, :] + total
        return 0

    lax.fori_loop(0, LANES // sub, body, 0, unroll=UNROLL)


def mean_weights(mean_coef, from_left, from_right, first, moved):
    rows = mean_coef.shape[0]
    depth = SWEEPS
    before = jnp.flip(from_left[4 : 4 + depth, first : first + rows].T, axis=1)
    after = from_right[4 : 4 + depth, first : first + rows].T
    wide = jnp.concatenate([before, mean_coef, after], axis=1)
    low = moved(wide[rows - depth :], "sx", 1)
    high = moved(wide[:depth], "sx", -1)
    win = jnp.concatenate([low, wide, high], axis=0)
    center = win[1:-1, 1:-1]
    near = (win[:-2, 1:-1], win[2:, 1:-1], win[1:-1, :-2], win[1:-1, 2:])
    near = [0.5 * (center + other) for other in near]
    diag = near[0] + near[1] + near[2] + near[3] + (react - theta)
    weights = jnp.stack([diag] + near) * (1.0 / delta)
    main = weights[:, :, 2:-2]
    side = jnp.concatenate([weights[:, :, :3], weights[:, :, -3:]], axis=2)
    side = jnp.transpose(side, (1, 0, 2)).reshape(rows + 4, 30)
    side = jnp.pad(side, ((1, 16 - rows - 5), (0, LANES - 30)))
    return main, side


def local(start_field, right_side, mean_coef, term_coef, coupling, block_mask):
    modes, width_x, width_y = start_field.shape
    terms = coupling.shape[0]
    owners = lax.axis_size("mode")
    blocks = block_mask.shape[1] // owners
    f = start_field.reshape(modes * width_x, width_y)
    rs = right_side.reshape(modes * width_x, width_y)
    term = term_coef.reshape(terms * width_x, width_y)

    def moved(value, axis, step):
        devices = lax.axis_size(axis)
        return lax.ppermute(value, axis, [(i, (i + step) % devices) for i in range(devices)])

    def shape(*dims):
        return jax.ShapeDtypeStruct(dims, f32)

    up, down, left, right = pl.pallas_call(
        functools.partial(pack_kernel, modes, terms),
        out_shape=(shape(modes + PAD, LANES),) * 2 + (shape(8, modes),) * 2,
        in_specs=[whole()] * 3,
        out_specs=(whole(),) * 4,
        compiler_params=params(),
        name="pack",
    )(f, mean_coef, term)
    from_left = moved(right, "sy", 1)
    from_right = moved(left, "sy", -1)
    low = moved(up, "sx", 1)
    high = moved(down, "sx", -1)

    chunks = CHUNKS if blocks % CHUNKS == 0 else 1
    part = blocks // chunks
    size = part * LANES
    segments = owners * chunks
    length, row_len = list_sizes(terms, blocks, part)
    lists = pl.pallas_call(
        functools.partial(list_kernel, segments, terms, blocks, part),
        out_shape=(
            jax.ShapeDtypeStruct((segments * length,), jnp.int32),
            jax.ShapeDtypeStruct((segments * row_len,), jnp.int32),
            jax.ShapeDtypeStruct((segments,), jnp.int32),
        ),
        in_specs=[smem()],
        out_specs=(smem(),) * 3,
        compiler_params=params(),
        name="lists",
    )(block_mask)

    def fluxes(rows, halos):
        operands = [f, *halos, from_left, from_right, mean_coef, term, rs]
        cfg = (modes, terms, rows, len(halos) > 0)
        halves = jax.ShapeDtypeStruct((terms * modes + LANES, 2 * LANES), bf16)
        return pl.pallas_call(
            functools.partial(flux_kernel, cfg),
            out_shape=(halves, halves, shape(2, modes, LANES)),
            in_specs=[whole()] * len(operands),
            out_specs=(whole(),) * 3,
            scratch_shapes=[
                pltpu.VMEM((2, 4, 16, LANES), f32),
                pltpu.VMEM((2, modes, LANES), f32),
                pltpu.VMEM((LANES, LANES), f32),
            ],
            compiler_params=params(),
            name="flux_edge" if halos else "flux_inner",
        )(*operands)

    def couple(halves, shift, chunk, base=None):
        own = base is not None
        operands = list(lists) + [coupling, *halves]
        specs = [smem()] * 3 + [pl.BlockSpec(memory_space=pl.ANY), whole(), whole()]
        if own:
            operands.append(base)
            specs.append(whole())
        cfg = (terms, blocks, owners, chunks, part, shift, chunk, own)
        return pl.pallas_call(
            functools.partial(couple_kernel, cfg),
            out_shape=shape(2, size, LANES),
            in_specs=specs,
            out_specs=whole(),
            scratch_shapes=[
                pltpu.VMEM((SLOTS, PAIR * GROUP, LANES, LANES), f32),
                pltpu.SemaphoreType.DMA((SLOTS,)),
            ],
            compiler_params=params(),
            cost_estimate=pl.CostEstimate(
                flops=3 * terms * modes * size * 2 * LANES,
                bytes_accessed=terms * modes * size * 2,
                transcendentals=0,
            ),
            name="couple_own" if own else "couple_other",
        )(*operands)

    def tie(value, *others):
        return lax.optimization_barrier((value, *others))[0]

    def coupled(halves, base):
        parts = [[couple(halves, s, c) for s in range(1, owners)] for c in range(chunks)]
        base = tie(base, *[p for ps in parts for p in ps])
        received = [[moved(p, "mode", s + 1) for s, p in enumerate(ps)] for ps in parts]
        own = []
        for c in range(chunks):
            own.append(couple(halves, 0, c, base))
            base = tie(base, own[-1])
        return own, received

    inner_high, inner_low, inner_base = fluxes((1, 2), ())
    inner, inner_parts = coupled((inner_high, inner_low), inner_base)
    low, high = lax.optimization_barrier((low, high, inner[-1]))[:2]
    for c in range(chunks):
        for value in inner_parts[c]:
            inner[c] = inner[c] - value
    low_in = [moved(v, "sx", 1) for v in inner]
    high_in = [moved(v, "sx", -1) for v in inner]
    edge_high, edge_low, edge_base = fluxes((0, 3), (low, high))
    edge, edge_parts = coupled((edge_high, edge_low), edge_base)

    main, corner = mean_weights(mean_coef, from_left, from_right, terms * width_x, moved)
    tiles = part
    ext = 8 * tiles
    pair = pl.BlockSpec((2, LANES, LANES), lambda k: (0, k, 0))
    row = pl.BlockSpec((LANES, LANES), lambda k: (k, 0))
    near = pl.BlockSpec((32, LANES), lambda k: (0, k))
    tail = pl.BlockSpec((ext, LANES), lambda k: (size // ext, 0))
    columns = pl.BlockSpec((32, size), lambda k: (0, 0))
    anywhere = pl.BlockSpec(memory_space=pl.ANY)

    def wide(c):
        return pl.BlockSpec((4 * LANES, LANES), lambda k: (c * tiles + k, 0))

    residual = None
    sends = []
    for c in range(chunks):
        operands = [inner[c], edge[c], *edge_parts[c]]
        specs = [pair] * len(operands)
        aliases = {}
        if c:
            aliases = {len(operands): 2}
            operands.append(residual)
            specs.append(anywhere)
        up, down, residual, side = pl.pallas_call(
            functools.partial(finish_kernel, len(edge_parts[c])),
            out_shape=(shape(size + ext, LANES),) * 2 + (shape(modes * 4, LANES), shape(32, size)),
            grid=(tiles,),
            in_specs=specs,
            out_specs=(row, row, wide(c), near),
            input_output_aliases=aliases,
            compiler_params=params(),
            name="finish",
        )(*operands)
        side_left = moved(side, "sy", 1)
        side_right = moved(side, "sy", -1)
        up, down = pl.pallas_call(
            functools.partial(extra_kernel, tiles),
            out_shape=(shape(size + ext, LANES),) * 2,
            grid=(1,),
            in_specs=[columns] * 3 + [anywhere] * 2,
            out_specs=(tail, tail),
            input_output_aliases={3: 0, 4: 1},
            compiler_params=params(),
            name="extra",
        )(side, side_left, side_right, up, down)
        sends.append((up, down, side, side_left, side_right, moved(up, "sx", 1), moved(down, "sx", -1)))

    solution = None
    for c in range(chunks):
        up, down, side, side_left, side_right, low, high = sends[c]
        operands = [f, inner[c], low_in[c], high_in[c], up, down, low, high, low, high]
        operands += [side, side_left, side_right, main, corner]
        specs = [wide(c), pair, pair, pair, row, row, row, row, tail, tail, columns, columns, columns]
        specs += [
            pl.BlockSpec((5, 8, LANES), lambda k: (0, 0, 0)),
            pl.BlockSpec((16, LANES), lambda k: (0, 0)),
        ]
        aliases = {}
        if c:
            aliases = {len(operands): 0}
            operands.append(solution)
            specs.append(anywhere)
        solution = pl.pallas_call(
            functools.partial(correct_kernel, size),
            out_shape=shape(modes * 4, LANES),
            grid=(tiles,),
            in_specs=specs,
            out_specs=wide(c),
            input_output_aliases=aliases,
            scratch_shapes=[
                pltpu.VMEM((10, 16, size), f32),
                pltpu.VMEM((LANES, size), f32),
                pltpu.VMEM((size, LANES), f32),
            ],
            compiler_params=params(),
            name="correct",
        )(*operands)
    full = (modes, width_x, width_y)
    return (solution.reshape(full), residual.reshape(full))


def solution(mesh):
    placed = (
        P("mode", "sx", "sy"),
        P("mode", "sx", "sy"),
        P("sx", "sy"),
        P(None, "sx", "sy"),
        P(None, None, "mode"),
        P(),
    )
    return jax.shard_map(
        local,
        mesh=mesh,
        in_specs=placed,
        out_specs=(P("mode", "sx", "sy"), P("mode", "sx", "sy")),
        check_vma=False,
    )
```

profile of v0, /device:TPU:0, one launch (start us, length us, event | category | flops | bytes accessed | tf_op | source)
XLA Modules:
  0.0 194.7 jit_solution(7342368510385280237)
XLA Ops:
  0.6 1.6 copy-done.4
  3.6 2.2 %pack.1 = (f32[1040,128]{1,0:T(8,128)}, f32[1040,128]{1,0:T(8,128)}, f32[8,1024]{1,0:T(8,128)S(1)}, f32[8,1024]{1,0:T(8,128)S(1)}) custom-call(f32[4096,128]{1,0:T(8,128)S(1)} %bitcast.21, f32[4,128]{1,0:T(4,128)S(1)} %copy-done.30, f32[32,128]{1,0:T(8,128)S(1)} %bitcast.28), custom_call_target="tpu_custom_call" | custom-call | tf_op jit(solution)/shard_map/pack/pallas_call | solution.py:489
  6.8 2.4 %collective-permute-start.1 = (f32[8,1024]{0,1:T(8,128)}, f32[8,1024]{0,1:T(8,128)S(1)}, u32[]{:S(2)}, u32[]{:S(2)}) collective-permute-start(f32[8,1024]{0,1:T(8,128)} %copy.22), channel_id=1, source_target_pairs={{0,3},{1,0},{2,1},{3,2},{4,7},{5,4},{6,5},{7,6},{8,11},{9,8},{10,9... | collective-permute-start | bytes 98312 | tf_op jit(solution)/shard_map/ppermute | solution.py:484
  10.2 1.6 collective-permute-start.5
  11.8 2.2 %collective-permute-start.6 = (f32[1040,128]{1,0:T(8,128)}, f32[1040,128]{1,0:T(8,128)}, u32[]{:S(2)}, u32[]{:S(2)}) collective-permute-start(f32[1040,128]{1,0:T(8,128)} %get-tuple-element.44), channel_id=1, source_target_pairs={{0,12},{4,0},{8,4},{12,8},{1,13},{5,1},{9,5},{13,9},{2,14},{6,2},{... | collective-permute-start | bytes 1597448 | tf_op jit(solution)/shard_map/ppermute | solution.py:484
  14.1 5.4 %lists.1 = (s32[1120]{0:T(1024)S(1)}, s32[168]{0:T(256)S(1)}, s32[4]{0:T(128)S(1)}) custom-call(s32[8,16,16]{2,1,0:T(8,128)S(1)} %copy-done.29), custom_call_target="tpu_custom_call" | custom-call | tf_op jit(solution)/shard_map/lists/pallas_call | solution.py:507
  21.0 1.9 collective-permute-done
  24.1 1.6 copy-done.6
  25.7 5.7 %flux_inner.1 = (bf16[8320,256]{1,0:T(8,128)(2,1)S(1)}, bf16[8320,256]{1,0:T(8,128)(2,1)S(1)}, f32[2,1024,128]{2,1,0:T(8,128)S(1)}) custom-call(f32[4096,128]{1,0:T(8,128)S(1)} %bitcast.22, f32[8,1024]{1,0:T(8,128)S(1)} %copy.23.refs_1_.refs_3_, f32[8,1024]{1,0:T(8,128)S(1)} %copy.24.refs_2_.refs_4_, f32[4,128]{1,0:T(4,128)S(1)} %copy-done.31, ...), custom_call_target="tpu_custom_call" | custom-call | tf_op jit(solution)/shard_map/flux_inner/pallas_call | solution.py:524
  31.4 9.0 %couple_other.5 = f32[2,512,128]{2,1,0:T(8,128)S(1)} custom-call(s32[1120]{0:T(1024)S(1)} %get-tuple-element.33.refs_0_, s32[168]{0:T(256)S(1)} %get-tuple-element.34.refs_1_, s32[4]{0:T(128)S(1)} %get-tuple-element.35.refs_2_, f32[8,2048,1024]{2,1,0:T(8,128)} %refs_3_.17, bf16[8320,256]{1,0:T(8,128)(2,1)S(1)} %get-tuple-element.38.refs_4_, ...), custom_call_target="tpu_custom_call" | custom-call | flops 3221225472 | bytes 8388608 | tf_op jit(solution)/shard_map/couple_other/pallas_call | solution.py:546
  40.4 9.2 %couple_other.4 = f32[2,512,128]{2,1,0:T(8,128)S(1)} custom-call(s32[1120]{0:T(1024)S(1)} %get-tuple-element.33.refs_0_, s32[168]{0:T(256)S(1)} %get-tuple-element.34.refs_1_, s32[4]{0:T(128)S(1)} %get-tuple-element.35.refs_2_, f32[8,2048,1024]{2,1,0:T(8,128)} %refs_3_.17, bf16[8320,256]{1,0:T(8,128)(2,1)S(1)} %get-tuple-element.38.refs_4_, ...), custom_call_target="tpu_custom_call" | custom-call | flops 3221225472 | bytes 8388608 | tf_op jit(solution)/shard_map/couple_other/pallas_call | solution.py:546
  53.7 2.2 %collective-permute-start.15 = (f32[3,134]{1,0:T(4,128)S(1)}, f32[3,134]{1,0:T(4,128)S(1)}, u32[]{:S(2)}, u32[]{:S(2)}) collective-permute-start(f32[3,134]{1,0:T(4,128)S(1)} %get-tuple-element.67), channel_id=1, source_target_pairs={{0,12},{4,0},{8,4},{12,8},{1,13},{5,1},{9,5},{13,9},{2,14},{6,2},{... | collective-permute-start | bytes 4832 | tf_op jit(solution)/shard_map/ppermute | solution.py:484
  56.0 2.4 %collective-permute-start.8 = (f32[2,512,128]{2,1,0:T(8,128)}, f32[2,512,128]{2,1,0:T(8,128)S(1)}, u32[]{:S(2)}, u32[]{:S(2)}) collective-permute-start(f32[2,512,128]{2,1,0:T(8,128)} %copy-done.12), channel_id=1, source_target_pairs={{0,16},{16,0},{1,17},{17,1},{2,18},{18,2},{3,19},{19,3},{4,20},{20... | collective-permute-start | bytes 1572872 | tf_op jit(solution)/shard_map/ppermute | solution.py:484
  58.3 2.2 %copy-done.1 = bf16[8320,256]{1,0:T(8,128)(2,1)S(1)} copy-done((bf16[8320,256]{1,0:T(8,128)(2,1)S(1)}, bf16[8320,256]{1,0:T(8,128)(2,1)}, u32[]{:S(2)}) %copy-start.1) | copy-done | bytes 4259864
  60.6 2.2 %copy-done.3 = bf16[8320,256]{1,0:T(8,128)(2,1)S(1)} copy-done((bf16[8320,256]{1,0:T(8,128)(2,1)S(1)}, bf16[8320,256]{1,0:T(8,128)(2,1)}, u32[]{:S(2)}) %copy-start.3) | copy-done | bytes 4259864
  62.8 9.5 %couple_own.4 = f32[2,512,128]{2,1,0:T(8,128)S(1)} custom-call(s32[1120]{0:T(1024)S(1)} %get-tuple-element.33.refs_0_, s32[168]{0:T(256)S(1)} %get-tuple-element.34.refs_1_, s32[4]{0:T(128)S(1)} %get-tuple-element.35.refs_2_, f32[8,2048,1024]{2,1,0:T(8,128)} %refs_3_.17, bf16[8320,256]{1,0:T(8,128)(2,1)S(1)} %copy-done.1, bf16[8320,256]{1,0:T(8,128)(2,1)S(1)} %copy-done.3, ...), custom_call_target="tpu_custom_call" | custom-call | flops 3221225472 | bytes 8388608 | tf_op jit(solution)/shard_map/couple_own/pallas_call | solution.py:546
  72.3 9.4 %couple_own.5 = f32[2,512,128]{2,1,0:T(8,128)S(1)} custom-call(s32[1120]{0:T(1024)S(1)} %get-tuple-element.33.refs_0_, s32[168]{0:T(256)S(1)} %get-tuple-element.34.refs_1_, s32[4]{0:T(128)S(1)} %get-tuple-element.35.refs_2_, f32[8,2048,1024]{2,1,0:T(8,128)} %refs_3_.17, bf16[8320,256]{1,0:T(8,128)(2,1)S(1)} %copy-done.1, bf16[8320,256]{1,0:T(8,128)(2,1)S(1)} %copy-done.3, ...), custom_call_target="tpu_custom_call" | custom-call | flops 3221225472 | bytes 8388608 | tf_op jit(solution)/shard_map/couple_own/pallas_call | solution.py:546
  82.2 6.9 %flux_edge.1 = (bf16[8320,256]{1,0:T(8,128)(2,1)S(1)}, bf16[8320,256]{1,0:T(8,128)(2,1)S(1)}, f32[2,1024,128]{2,1,0:T(8,128)S(1)}) custom-call(f32[4096,128]{1,0:T(8,128)S(1)} %bitcast.23, f32[1040,128]{1,0:T(8,128)} %collective-permute-done.5.refs_1_, f32[1040,128]{1,0:T(8,128)} %collective-permute-done.6.refs_2_, f32[8,1024]{1,0:T(8,128)S(1)} %copy.23.refs_1_.refs_3_, ...), custom_call_target="tpu_custom_call" | custom-call | tf_op jit(solution)/shard_map/flux_edge/pallas_call | solution.py:524
  89.2 9.2 %couple_other.6 = f32[2,512,128]{2,1,0:T(8,128)S(1)} custom-call(s32[1120]{0:T(1024)S(1)} %get-tuple-element.33.refs_0_, s32[168]{0:T(256)S(1)} %get-tuple-element.34.refs_1_, s32[4]{0:T(128)S(1)} %get-tuple-element.35.refs_2_, f32[8,2048,1024]{2,1,0:T(8,128)} %refs_3_.17, bf16[8320,256]{1,0:T(8,128)(2,1)S(1)} %get-tuple-element.47.refs_4_, ...), custom_call_target="tpu_custom_call" | custom-call | flops 3221225472 | bytes 8388608 | tf_op jit(solution)/shard_map/couple_other/pallas_call | solution.py:546
  98.4 2.1 %collective-permute-start.9 = (f32[2,512,128]{2,1,0:T(8,128)S(1)}, f32[2,512,128]{2,1,0:T(8,128)S(1)}, u32[]{:S(2)}, u32[]{:S(2)}) collective-permute-start(f32[2,512,128]{2,1,0:T(8,128)S(1)} %couple_other.6), channel_id=1, source_target_pairs={{0,16},{16,0},{1,17},{17,1},{2,18},{18,2},{3,19},{19,3},{4,20},{20... | collective-permute-start | bytes 1572872 | tf_op jit(solution)/shard_map/ppermute | solution.py:484
  100.5 7.6 %couple_other.7 = f32[2,512,128]{2,1,0:T(8,128)S(1)} custom-call(s32[1120]{0:T(1024)S(1)} %get-tuple-element.33.refs_0_, s32[168]{0:T(256)S(1)} %get-tuple-element.34.refs_1_, s32[4]{0:T(128)S(1)} %get-tuple-element.35.refs_2_, f32[8,2048,1024]{2,1,0:T(8,128)} %refs_3_.17, bf16[8320,256]{1,0:T(8,128)(2,1)S(1)} %get-tuple-element.47.refs_4_, ...), custom_call_target="tpu_custom_call" | custom-call | flops 3221225472 | bytes 8388608 | tf_op jit(solution)/shard_map/couple_other/pallas_call | solution.py:546
  109.1 9.5 %couple_own.6.base_ref = f32[2,512,128]{2,1,0:T(8,128)S(1)} custom-call(s32[1120]{0:T(1024)S(1)} %get-tuple-element.33.refs_0_, s32[168]{0:T(256)S(1)} %get-tuple-element.34.refs_1_, s32[4]{0:T(128)S(1)} %get-tuple-element.35.refs_2_, f32[8,2048,1024]{2,1,0:T(8,128)} %refs_3_.17, bf16[8320,256]{1,0:T(8,128)(2,1)S(1)} %get-tuple-element.47.refs_4_, ...), custom_call_target="tpu_custom_call" | custom-call | flops 3221225472 | bytes 8388608 | tf_op jit(solution)/shard_map/couple_own/pallas_call | solution.py:546
  118.7 1.8 collective-permute-start.17
  120.8 2.2 %finish.2 = (f32[544,128]{1,0:T(8,128)S(1)}, f32[544,128]{1,0:T(8,128)}, f32[4096,128]{1,0:T(8,128)}, f32[32,512]{1,0:T(8,128)S(1)}) custom-call(f32[2,512,128]{2,1,0:T(8,128)S(1)} %sub.7.inner_ref, f32[2,512,128]{2,1,0:T(8,128)S(1)} %couple_own.6.base_ref, f32[2,512,128]{2,1,0:T(8,128)S(1)} %collective-permute-done.9.refs_0_), custom_call_target="tpu_custom_call" | custom-call | tf_op jit(solution)/shard_map/finish/pallas_call | solution.py:611
  123.5 9.5 %couple_own.7.base_ref = f32[2,512,128]{2,1,0:T(8,128)S(1)} custom-call(s32[1120]{0:T(1024)S(1)} %get-tuple-element.33.refs_0_, s32[168]{0:T(256)S(1)} %get-tuple-element.34.refs_1_, s32[4]{0:T(128)S(1)} %get-tuple-element.35.refs_2_, f32[8,2048,1024]{2,1,0:T(8,128)} %refs_3_.17, bf16[8320,256]{1,0:T(8,128)(2,1)S(1)} %get-tuple-element.47.refs_4_, ...), custom_call_target="tpu_custom_call" | custom-call | flops 3221225472 | bytes 8388608 | tf_op jit(solution)/shard_map/couple_own/pallas_call | solution.py:546
  133.1 2.3 %finish.3 = (f32[544,128]{1,0:T(8,128)}, f32[544,128]{1,0:T(8,128)}, f32[4096,128]{1,0:T(8,128)}, f32[32,512]{1,0:T(8,128)S(1)}) custom-call(f32[2,512,128]{2,1,0:T(8,128)S(1)} %sub.6.inner_ref, f32[2,512,128]{2,1,0:T(8,128)S(1)} %couple_own.7.base_ref, f32[2,512,128]{2,1,0:T(8,128)S(1)} %collective-permute-done.7.refs_0_, ...), custom_call_target="tpu_custom_call", output_to_operand_aliasing={{2}: (3, {})} | custom-call | tf_op jit(solution)/shard_map/finish/pallas_call | solution.py:611
  138.5 3.5 %collective-permute-start.4 = (f32[2,512,128]{2,1,0:T(8,128)S(1)}, f32[2,512,128]{2,1,0:T(8,128)}, u32[]{:S(2)}, u32[]{:S(2)}) collective-permute-start(f32[2,512,128]{2,1,0:T(8,128)S(1)} %sub.6.inner_ref), channel_id=1, source_target_pairs={{0,12},{4,0},{8,4},{12,8},{1,13},{5,1},{9,5},{13,9},{2,14},{6,2},{... | collective-permute-start | bytes 1572872 | tf_op jit(solution)/shard_map/ppermute | solution.py:484
  144.2 3.8 %collective-permute-start.21 = (f32[544,128]{1,0:T(8,128)}, f32[544,128]{1,0:T(8,128)}, u32[]{:S(2)}, u32[]{:S(2)}) collective-permute-start(f32[544,128]{1,0:T(8,128)} %get-tuple-element.62.down_ref), channel_id=1, source_target_pairs={{0,12},{4,0},{8,4},{12,8},{1,13},{5,1},{9,5},{13,9},{2,14},{6,2},{... | collective-permute-start | bytes 835592 | tf_op jit(solution)/shard_map/ppermute | solution.py:484
  148.8 3.9 %collective-permute-start.13 = (f32[544,128]{1,0:T(8,128)}, f32[544,128]{1,0:T(8,128)}, u32[]{:S(2)}, u32[]{:S(2)}) collective-permute-start(f32[544,128]{1,0:T(8,128)} %get-tuple-element.57.down_ref), channel_id=1, source_target_pairs={{0,12},{4,0},{8,4},{12,8},{1,13},{5,1},{9,5},{13,9},{2,14},{6,2},{... | collective-permute-start | bytes 835592 | tf_op jit(solution)/shard_map/ppermute | solution.py:484
  155.6 21.4 %collective-permute-done.21.high_ref.high_x_ref = f32[544,128]{1,0:T(8,128)} collective-permute-done((f32[544,128]{1,0:T(8,128)}, f32[544,128]{1,0:T(8,128)}, u32[]{:S(2)}, u32[]{:S(2)}) %collective-permute-start.21) | collective-permute-done | bytes 278560 | tf_op jit(solution)/shard_map/ppermute | solution.py:484
  181.6 6.5 %correct.2.refs_0_ = f32[4096,128]{1,0:T(8,128)} custom-call(f32[4096,128]{1,0:T(8,128)S(1)} %bitcast.24, f32[2,512,128]{2,1,0:T(8,128)S(1)} %sub.7.inner_ref, f32[2,512,128]{2,1,0:T(8,128)S(1)} %copy-done.16, f32[2,512,128]{2,1,0:T(8,128)S(1)} %copy-done.14, f32[544,128]{1,0:T(8,128)S(1)} %copy-done.9, f32[544,128]{1,0:T(8,128)} %get-tuple-element.62.down_ref, ...), custom_call_target="tpu_custom_call" | custom-call | tf_op jit(solution)/shard_map/correct/pallas_call | solution.py:650
  188.1 6.6 %correct.3 = f32[4096,128]{1,0:T(8,128)} custom-call(f32[4096,128]{1,0:T(8,128)S(1)} %bitcast.25, f32[2,512,128]{2,1,0:T(8,128)S(1)} %sub.6.inner_ref, f32[2,512,128]{2,1,0:T(8,128)} %collective-permute-done.3.low_in_ref, f32[2,512,128]{2,1,0:T(8,128)} %collective-permute-done.4.high_in_ref, ...), custom_call_target="tpu_custom_call", output_to_operand_aliasing={{}: (15, {})} | custom-call | tf_op jit(solution)/shard_map/correct/pallas_call | solution.py:650
  (120 shorter events, 26.2 us)
Async XLA Ops:
  3.6 10.4 %copy-start.29 = (s32[8,16,16]{2,1,0:T(8,128)S(1)}, s32[8,16,16]{2,1,0:T(8,128)}, u32[]{:S(2)}) copy-start(s32[8,16,16]{2,1,0:T(8,128)} %mask_ref.1) | copy-start | bytes 24580
  3.6 20.5 %copy-start.5 = (f32[1024,4,128]{2,1,0:T(4,128)S(1)}, f32[1024,4,128]{2,1,0:T(4,128)}, u32[]{:S(2)}) copy-start(f32[1024,4,128]{2,1,0:T(4,128)} %param.6) | copy-start | bytes 6291460
  3.6 20.5 %copy-start.28 = (f32[8,4,128]{2,1,0:T(4,128)S(1)}, f32[8,4,128]{2,1,0:T(4,128)}, u32[]{:S(2)}) copy-start(f32[8,4,128]{2,1,0:T(4,128)} %param.9) | copy-start | bytes 49156
  3.6 20.5 %copy-start.31 = (f32[4,128]{1,0:T(4,128)S(1)}, f32[4,128]{1,0:T(4,128)}, u32[]{:S(2)}) copy-start(f32[4,128]{1,0:T(4,128)} %refs_5_.1) | copy-start | bytes 6148
  6.8 14.0 %collective-permute-start.1 = (f32[8,1024]{0,1:T(8,128)}, f32[8,1024]{0,1:T(8,128)S(1)}, u32[]{:S(2)}, u32[]{:S(2)}) collective-permute-start(f32[8,1024]{0,1:T(8,128)} %copy.22), channel_id=1, source_target_pairs={{0,3},{1,0},{2,1},{3,2},{4,7},{5,4},{6,5},{7,6},{8,11},{9,8},{10,9... | collective-permute-start | bytes 98312 | tf_op jit(solution)/shard_map/ppermute | solution.py:484
  10.2 12.6 %collective-permute-start = (f32[8,1024]{0,1:T(8,128)}, f32[8,1024]{0,1:T(8,128)}, u32[]{:S(2)}, u32[]{:S(2)}) collective-permute-start(f32[8,1024]{0,1:T(8,128)} %copy.21), channel_id=1, source_target_pairs={{0,1},{1,2},{2,3},{3,0},{4,5},{5,6},{6,7},{7,4},{8,9},{9,10},{10,1... | collective-permute-start | bytes 98312 | tf_op jit(solution)/shard_map/ppermute | solution.py:484
  10.2 72.0 %collective-permute-start.5 = (f32[1040,128]{1,0:T(8,128)}, f32[1040,128]{1,0:T(8,128)}, u32[]{:S(2)}, u32[]{:S(2)}) collective-permute-start(f32[1040,128]{1,0:T(8,128)} %get-tuple-element.43), channel_id=1, source_target_pairs={{0,4},{4,8},{8,12},{12,0},{1,5},{5,9},{9,13},{13,1},{2,6},{6,10},{... | collective-permute-start | bytes 1597448 | tf_op jit(solution)/shard_map/ppermute | solution.py:484
  11.8 70.4 %collective-permute-start.6 = (f32[1040,128]{1,0:T(8,128)}, f32[1040,128]{1,0:T(8,128)}, u32[]{:S(2)}, u32[]{:S(2)}) collective-permute-start(f32[1040,128]{1,0:T(8,128)} %get-tuple-element.44), channel_id=1, source_target_pairs={{0,12},{4,0},{8,4},{12,8},{1,13},{5,1},{9,5},{13,9},{2,14},{6,2},{... | collective-permute-start | bytes 1597448 | tf_op jit(solution)/shard_map/ppermute | solution.py:484
  52.1 29.6 %collective-permute-start.14 = (f32[3,134]{1,0:T(4,128)S(1)}, f32[3,134]{1,0:T(4,128)S(1)}, u32[]{:S(2)}, u32[]{:S(2)}) collective-permute-start(f32[3,134]{1,0:T(4,128)S(1)} %get-tuple-element.66), channel_id=1, source_target_pairs={{0,4},{4,8},{8,12},{12,0},{1,5},{5,9},{9,13},{13,1},{2,6},{6,10},{... | collective-permute-start | bytes 4832 | tf_op jit(solution)/shard_map/ppermute | solution.py:484
  53.7 28.1 %collective-permute-start.15 = (f32[3,134]{1,0:T(4,128)S(1)}, f32[3,134]{1,0:T(4,128)S(1)}, u32[]{:S(2)}, u32[]{:S(2)}) collective-permute-start(f32[3,134]{1,0:T(4,128)S(1)} %get-tuple-element.67), channel_id=1, source_target_pairs={{0,12},{4,0},{8,4},{12,8},{1,13},{5,1},{9,5},{13,9},{2,14},{6,2},{... | collective-permute-start | bytes 4832 | tf_op jit(solution)/shard_map/ppermute | solution.py:484
  56.0 62.7 %collective-permute-start.8 = (f32[2,512,128]{2,1,0:T(8,128)}, f32[2,512,128]{2,1,0:T(8,128)S(1)}, u32[]{:S(2)}, u32[]{:S(2)}) collective-permute-start(f32[2,512,128]{2,1,0:T(8,128)} %copy-done.12), channel_id=1, source_target_pairs={{0,16},{16,0},{1,17},{17,1},{2,18},{18,2},{3,19},{19,3},{4,20},{20... | collective-permute-start | bytes 1572872 | tf_op jit(solution)/shard_map/ppermute | solution.py:484
  72.3 9.4 %copy-start.11 = (f32[2,512,128]{2,1,0:T(8,128)S(1)}, f32[2,512,128]{2,1,0:T(8,128)}, u32[]{:S(2)}) copy-start(f32[2,512,128]{2,1,0:T(8,128)} %copy-done.10) | copy-start | bytes 1572868
  72.3 9.9 %copy-start.7 = (f32[1024,4,128]{2,1,0:T(4,128)S(1)}, f32[1024,4,128]{2,1,0:T(4,128)}, u32[]{:S(2)}) copy-start(f32[1024,4,128]{2,1,0:T(4,128)} %param.7) | copy-start | bytes 6291460
  81.7 41.3 %collective-permute-start.2 = (f32[2,512,128]{2,1,0:T(8,128)S(1)}, f32[2,512,128]{2,1,0:T(8,128)S(1)}, u32[]{:S(2)}, u32[]{:S(2)}) collective-permute-start(f32[2,512,128]{2,1,0:T(8,128)S(1)} %copy-done.11), channel_id=1, source_target_pairs={{0,16},{16,0},{1,17},{17,1},{2,18},{18,2},{3,19},{19,3},{4,20},{20... | collective-permute-start | bytes 1572872 | tf_op jit(solution)/shard_map/ppermute | solution.py:484
  98.4 22.4 %collective-permute-start.9 = (f32[2,512,128]{2,1,0:T(8,128)S(1)}, f32[2,512,128]{2,1,0:T(8,128)S(1)}, u32[]{:S(2)}, u32[]{:S(2)}) collective-permute-start(f32[2,512,128]{2,1,0:T(8,128)S(1)} %couple_other.6), channel_id=1, source_target_pairs={{0,16},{16,0},{1,17},{17,1},{2,18},{18,2},{3,19},{19,3},{4,20},{20... | collective-permute-start | bytes 1572872 | tf_op jit(solution)/shard_map/ppermute | solution.py:484
  108.1 25.0 %collective-permute-start.7 = (f32[2,512,128]{2,1,0:T(8,128)S(1)}, f32[2,512,128]{2,1,0:T(8,128)S(1)}, u32[]{:S(2)}, u32[]{:S(2)}) collective-permute-start(f32[2,512,128]{2,1,0:T(8,128)S(1)} %couple_other.7), channel_id=1, source_target_pairs={{0,16},{16,0},{1,17},{17,1},{2,18},{18,2},{3,19},{19,3},{4,20},{20... | collective-permute-start | bytes 1572872 | tf_op jit(solution)/shard_map/ppermute | solution.py:484
  118.7 24.7 %collective-permute-start.17 = (f32[2,512,128]{2,1,0:T(8,128)S(1)}, f32[2,512,128]{2,1,0:T(8,128)S(1)}, u32[]{:S(2)}, u32[]{:S(2)}) collective-permute-start(f32[2,512,128]{2,1,0:T(8,128)S(1)} %sub.7.inner_ref), channel_id=1, source_target_pairs={{0,12},{4,0},{8,4},{12,8},{1,13},{5,1},{9,5},{13,9},{2,14},{6,2},{... | collective-permute-start | bytes 1572872 | tf_op jit(solution)/shard_map/ppermute | solution.py:484
  120.5 27.5 %collective-permute-start.16 = (f32[2,512,128]{2,1,0:T(8,128)S(1)}, f32[2,512,128]{2,1,0:T(8,128)S(1)}, u32[]{:S(2)}, u32[]{:S(2)}) collective-permute-start(f32[2,512,128]{2,1,0:T(8,128)S(1)} %sub.7.inner_ref), channel_id=1, source_target_pairs={{0,4},{4,8},{8,12},{12,0},{1,5},{5,9},{9,13},{13,1},{2,6},{6,10},{... | collective-permute-start | bytes 1572872 | tf_op jit(solution)/shard_map/ppermute | solution.py:484
  123.0 13.6 %collective-permute-start.19 = (f32[32,512]{1,0:T(8,128)S(1)}, f32[32,512]{1,0:T(8,128)S(1)}, u32[]{:S(2)}, u32[]{:S(2)}) collective-permute-start(f32[32,512]{1,0:T(8,128)S(1)} %get-tuple-element.58.side_ref), channel_id=1, source_target_pairs={{0,3},{1,0},{2,1},{3,2},{4,7},{5,4},{6,5},{7,6},{8,11},{9,8},{10,9... | collective-permute-start | bytes 196616 | tf_op jit(solution)/shard_map/ppermute | solution.py:484
  123.0 13.6 %collective-permute-start.18 = (f32[32,512]{1,0:T(8,128)S(1)}, f32[32,512]{1,0:T(8,128)S(1)}, u32[]{:S(2)}, u32[]{:S(2)}) collective-permute-start(f32[32,512]{1,0:T(8,128)S(1)} %get-tuple-element.58.side_ref), channel_id=1, source_target_pairs={{0,1},{1,2},{2,3},{3,0},{4,5},{5,6},{6,7},{7,4},{8,9},{9,10},{10,1... | collective-permute-start | bytes 196616 | tf_op jit(solution)/shard_map/ppermute | solution.py:484
  135.3 13.5 %copy-start.17 = (f32[32,512]{1,0:T(8,128)}, f32[32,512]{1,0:T(8,128)S(1)}, u32[]{:S(2)}) copy-start(f32[32,512]{1,0:T(8,128)S(1)} %get-tuple-element.53.side_ref) | copy-start | bytes 196612
  135.3 3.2 %collective-permute-start.11 = (f32[32,512]{1,0:T(8,128)S(1)}, f32[32,512]{1,0:T(8,128)S(1)}, u32[]{:S(2)}, u32[]{:S(2)}) collective-permute-start(f32[32,512]{1,0:T(8,128)S(1)} %get-tuple-element.53.side_ref), channel_id=1, source_target_pairs={{0,3},{1,0},{2,1},{3,2},{4,7},{5,4},{6,5},{7,6},{8,11},{9,8},{10,9... | collective-permute-start | bytes 196616 | tf_op jit(solution)/shard_map/ppermute | solution.py:484
  136.6 5.5 %collective-permute-start.10 = (f32[32,512]{1,0:T(8,128)S(1)}, f32[32,512]{1,0:T(8,128)S(1)}, u32[]{:S(2)}, u32[]{:S(2)}) collective-permute-start(f32[32,512]{1,0:T(8,128)S(1)} %get-tuple-element.53.side_ref), channel_id=1, source_target_pairs={{0,1},{1,2},{2,3},{3,0},{4,5},{5,6},{6,7},{7,4},{8,9},{9,10},{10,1... | collective-permute-start | bytes 196616 | tf_op jit(solution)/shard_map/ppermute | solution.py:484
  137.3 11.6 %copy-start.8 = (f32[544,128]{1,0:T(8,128)}, f32[544,128]{1,0:T(8,128)S(1)}, u32[]{:S(2)}) copy-start(f32[544,128]{1,0:T(8,128)S(1)} %get-tuple-element.61.up_ref) | copy-start | bytes 835588
  137.3 11.5 %collective-permute-start.20 = (f32[544,128]{1,0:T(8,128)S(1)}, f32[544,128]{1,0:T(8,128)S(1)}, u32[]{:S(2)}, u32[]{:S(2)}) collective-permute-start(f32[544,128]{1,0:T(8,128)S(1)} %get-tuple-element.61.up_ref), channel_id=1, source_target_pairs={{0,4},{4,8},{8,12},{12,0},{1,5},{5,9},{9,13},{13,1},{2,6},{6,10},{... | collective-permute-start | bytes 835592 | tf_op jit(solution)/shard_map/ppermute | solution.py:484
  138.5 14.2 %copy-start.21 = (f32[32,512]{1,0:T(8,128)}, f32[32,512]{1,0:T(8,128)S(1)}, u32[]{:S(2)}) copy-start(f32[32,512]{1,0:T(8,128)S(1)} %collective-permute-done.11.right_ref) | copy-start | bytes 196612
  138.5 49.5 %collective-permute-start.4 = (f32[2,512,128]{2,1,0:T(8,128)S(1)}, f32[2,512,128]{2,1,0:T(8,128)}, u32[]{:S(2)}, u32[]{:S(2)}) collective-permute-start(f32[2,512,128]{2,1,0:T(8,128)S(1)} %sub.6.inner_ref), channel_id=1, source_target_pairs={{0,12},{4,0},{8,4},{12,8},{1,13},{5,1},{9,5},{13,9},{2,14},{6,2},{... | collective-permute-start | bytes 1572872 | tf_op jit(solution)/shard_map/ppermute | solution.py:484
  142.1 10.7 %copy-start.23 = (f32[32,512]{1,0:T(8,128)}, f32[32,512]{1,0:T(8,128)S(1)}, u32[]{:S(2)}) copy-start(f32[32,512]{1,0:T(8,128)S(1)} %collective-permute-done.10.left_ref) | copy-start | bytes 196612
  142.1 46.0 %collective-permute-start.3 = (f32[2,512,128]{2,1,0:T(8,128)S(1)}, f32[2,512,128]{2,1,0:T(8,128)}, u32[]{:S(2)}, u32[]{:S(2)}) collective-permute-start(f32[2,512,128]{2,1,0:T(8,128)S(1)} %sub.6.inner_ref), channel_id=1, source_target_pairs={{0,4},{4,8},{8,12},{12,0},{1,5},{5,9},{9,13},{13,1},{2,6},{6,10},{... | collective-permute-start | bytes 1572872 | tf_op jit(solution)/shard_map/ppermute | solution.py:484
  144.2 32.7 %collective-permute-start.21 = (f32[544,128]{1,0:T(8,128)}, f32[544,128]{1,0:T(8,128)}, u32[]{:S(2)}, u32[]{:S(2)}) collective-permute-start(f32[544,128]{1,0:T(8,128)} %get-tuple-element.62.down_ref), channel_id=1, source_target_pairs={{0,12},{4,0},{8,4},{12,8},{1,13},{5,1},{9,5},{13,9},{2,14},{6,2},{... | collective-permute-start | bytes 835592 | tf_op jit(solution)/shard_map/ppermute | solution.py:484
  148.8 39.2 %collective-permute-start.12 = (f32[544,128]{1,0:T(8,128)}, f32[544,128]{1,0:T(8,128)}, u32[]{:S(2)}, u32[]{:S(2)}) collective-permute-start(f32[544,128]{1,0:T(8,128)} %get-tuple-element.56.up_ref), channel_id=1, source_target_pairs={{0,4},{4,8},{8,12},{12,0},{1,5},{5,9},{9,13},{13,1},{2,6},{6,10},{... | collective-permute-start | bytes 835592 | tf_op jit(solution)/shard_map/ppermute | solution.py:484
  148.8 39.2 %collective-permute-start.13 = (f32[544,128]{1,0:T(8,128)}, f32[544,128]{1,0:T(8,128)}, u32[]{:S(2)}, u32[]{:S(2)}) collective-permute-start(f32[544,128]{1,0:T(8,128)} %get-tuple-element.57.down_ref), channel_id=1, source_target_pairs={{0,12},{4,0},{8,4},{12,8},{1,13},{5,1},{9,5},{13,9},{2,14},{6,2},{... | collective-permute-start | bytes 835592 | tf_op jit(solution)/shard_map/ppermute | solution.py:484
  (23 other events, 73.2 us)
where the time goes:
time: 198 us; the launch traced here: 195 us
  Pallas kernels  112 us (57%)
  starting transfers between devices  30.8 us (16%)
  waiting for transfers between devices  25.8 us (13%)
  local copies, waits for them, and re-layouts  24.5 us (12%)
    pallas_call x8, Pallas kernels, couple(): pl.pallas_call(functools.partial(couple_kernel, cfg), out_shape=shape(2,...  72.9 us
    ppermute x22, starting transfers between devices, moved(): lax.ppermute(value, axis, [(i, (i + step) % devices) for i in range(devic...  30.8 us
    ppermute x22, waiting for transfers between devices, moved(): lax.ppermute(value, axis, [(i, (i + step) % devices) for i in range(devic...  25.8 us
    unnamed x66, local copies, waits for them, and re-layouts  16 us
    pallas_call x2, Pallas kernels, local(): pl.pallas_call(functools.partial(correct_kernel, size), out_shape=shape(m...  13.1 us
    pallas_call x2, Pallas kernels, fluxes(): pl.pallas_call(functools.partial(flux_kernel, cfg), out_shape=(halves, ha...  12.6 us
    pallas_call x1, Pallas kernels, local(): pl.pallas_call(functools.partial(list_kernel, segments, terms, blocks, pa...  5.44 us
    pallas_call x2, Pallas kernels, local(): pl.pallas_call(functools.partial(finish_kernel, len(edge_parts[c])), out_...  4.45 us
  transfers between devices with their start and end apart: 22, of which 4 were waited for; matrix products, arithmetic and copies ran while one was open for 4% of the time, Pallas kernels for 53%

commit v1 on v0

--- a/solution.py
+++ b/solution.py
@@ -22,6 +22,8 @@
 SUB = 32
 UNROLL = 4
 VMEM_LIMIT = 24 * 1024 * 1024
+
+LITTLE = pl.CostEstimate(flops=1024, bytes_accessed=1024, transcendentals=0)
 
 f32 = jnp.float32
 bf16 = jnp.bfloat16
@@ -80,7 +82,8 @@
     for ref, x in ((up_ref, 3), (down_ref, 0)):
         ref[modes : modes + terms, :] = term_ref[pl.ds(x, terms, stride=4), :]
         ref[modes + terms : modes + terms + 1, :] = mean_ref[x : x + 1, :]
-        ref[modes + terms + 1 : modes + PAD, :] = jnp.zeros((PAD - terms - 1, LANES), f32)
+        ref[modes + terms + 1 : modes + terms + 5, :] = mean_ref[...]
+        ref[modes + terms + 5 : modes + PAD, :] = jnp.zeros((PAD - terms - 5, LANES), f32)
     shape = (LANES, LANES)
     lane = lane_iota(shape)
     for m in range(modes // LANES):
@@ -95,9 +98,8 @@
     rows = terms * 4
     coefs = jnp.concatenate([term_ref[...], mean_ref[...], jnp.zeros((LANES - rows - 4, LANES), f32)], axis=0)
     turned = coefs.T
-    for k in range(SWEEPS):
-        left_ref[4 + k : 5 + k, 0:LANES] = turned[k : k + 1, :]
-        right_ref[4 + k : 5 + k, 0:LANES] = turned[LANES - 1 - k : LANES - k, :]
+    left_ref[4:5, 0:LANES] = turned[0:1, :]
+    right_ref[4:5, 0:LANES] = turned[LANES - 1 : LANES, :]
 
 
 def list_sizes(terms, blocks, part):
@@ -237,7 +239,7 @@
 
 
 def couple_kernel(cfg, *refs):
-    terms, blocks, owners, chunks, part, shift, chunk, own = cfg
+    terms, blocks, owners, chunks, part, shift, first, count, own = cfg
     refs = list(refs)
     list_ref, row_ref, count_ref, a_ref, fh_ref, fl_ref = refs[:6]
     refs = refs[6:]
@@ -246,80 +248,93 @@
     out_ref, slot_ref, sem = refs
     length, row_len = list_sizes(terms, blocks, part)
     owner = lax.rem(lax.axis_index("mode") + shift, owners)
-    segment = owner * chunks + chunk
-    steps = count_ref[segment]
     none = terms * blocks
     step_blocks = PAIR * GROUP
 
-    def fetch(step, slot):
-        for p in range(PAIR):
-            a = row_ref[segment * row_len + step * PAIR + p]
-            row = pl.multiple_of(((owner * chunks + chunk) * part + a) * LANES, LANES)
-            for k in range(p * GROUP, (p + 1) * GROUP):
-                e = jnp.minimum(list_ref[segment * length + step * step_blocks + k], none - 1)
-                t = e // blocks
-                b = e - t * blocks
-                pltpu.make_async_copy(
-                    a_ref.at[t, pl.ds(row, LANES), pl.ds(pl.multiple_of(b * LANES, LANES), LANES)],
-                    slot_ref.at[slot, k],
-                    sem.at[slot],
-                ).start()
-
-    for i in range(SLOTS - 1):
-        @pl.when(i < steps)
-        def _():
-            fetch(i, i)
-
     if own:
-        out_ref[...] = base_ref[:, chunk * part * LANES : (chunk + 1) * part * LANES, :]
+        out_ref[...] = base_ref[:, first * part * LANES : (first + count) * part * LANES, :]
     else:
         out_ref[...] = jnp.zeros(out_ref.shape, f32)
 
-    def product(step, _):
-        slot = lax.rem(step, SLOTS)
-
-        @pl.when(step + SLOTS - 1 < steps)
-        def _():
-            fetch(step + SLOTS - 1, lax.rem(step + SLOTS - 1, SLOTS))
-
-        pltpu.make_async_copy(slot_ref.at[slot], slot_ref.at[slot], sem.at[slot]).wait()
-        for p in range(PAIR):
-            highs, lows, fhs, fls = [], [], [], []
-            for k in range(p * GROUP, (p + 1) * GROUP):
-                block = slot_ref[slot, k]
-                high = block.astype(bf16)
-                highs.append(high)
-                lows.append((block - high.astype(f32)).astype(bf16))
-                at = pl.multiple_of(list_ref[segment * length + step * step_blocks + k] * LANES, LANES)
-                fhs.append(fh_ref[pl.ds(at, LANES), :])
-                fls.append(fl_ref[pl.ds(at, LANES), :])
-            high = jnp.concatenate(highs, axis=1)
-            low = jnp.concatenate(lows, axis=1)
-            fh = jnp.concatenate(fhs, axis=0)
-            fl = jnp.concatenate(fls, axis=0)
-            both = jnp.dot(jnp.concatenate([high, low], axis=0), fh, preferred_element_type=f32)
-            total = both[:LANES] + both[LANES:] + jnp.dot(high, fl, preferred_element_type=f32)
-            to = pl.ds(pl.multiple_of(row_ref[segment * row_len + step * PAIR + p] * LANES, LANES), LANES)
-            for i in range(2):
-                piece = total[:, i * LANES : (i + 1) * LANES]
-                if own:
-                    out_ref[i, to, :] = out_ref[i, to, :] - piece
-                else:
-                    out_ref[i, to, :] = out_ref[i, to, :] + piece
+    def per_chunk(chunk, _):
+        segment = owner * chunks + first + chunk
+        steps = count_ref[segment]
+
+        def fetch(step, slot):
+            for p in range(PAIR):
+                a = row_ref[segment * row_len + step * PAIR + p]
+                row = pl.multiple_of((segment * part + a) * LANES, LANES)
+                for k in range(p * GROUP, (p + 1) * GROUP):
+                    e = jnp.minimum(list_ref[segment * length + step * step_blocks + k], none - 1)
+                    t = e // blocks
+                    b = e - t * blocks
+                    pltpu.make_async_copy(
+                        a_ref.at[t, pl.ds(row, LANES), pl.ds(pl.multiple_of(b * LANES, LANES), LANES)],
+                        slot_ref.at[slot, k],
+                        sem.at[slot],
+                    ).start()
+
+        for i in range(SLOTS - 1):
+            @pl.when(i < steps)
+            def _():
+                fetch(i, i)
+
+        def product(step, _):
+            slot = lax.rem(step, SLOTS)
+
+            @pl.when(step + SLOTS - 1 < steps)
+            def _():
+                fetch(step + SLOTS - 1, lax.rem(step + SLOTS - 1, SLOTS))
+
+            pltpu.make_async_copy(slot_ref.at[slot], slot_ref.at[slot], sem.at[slot]).wait()
+            for p in range(PAIR):
+                highs, lows, fhs, fls = [], [], [], []
+                for k in range(p * GROUP, (p + 1) * GROUP):
+                    block = slot_ref[slot, k]
+                    high = block.astype(bf16)
+                    highs.append(high)
+                    lows.append((block - high.astype(f32)).astype(bf16))
+                    at = pl.multiple_of(list_ref[segment * length + step * step_blocks + k] * LANES, LANES)
+                    fhs.append(fh_ref[pl.ds(at, LANES), :])
+                    fls.append(fl_ref[pl.ds(at, LANES), :])
+                high = jnp.concatenate(highs, axis=1)
+                low = jnp.concatenate(lows, axis=1)
+                fh = jnp.concatenate(fhs, axis=0)
+                fl = jnp.concatenate(fls, axis=0)
+                both = jnp.dot(jnp.concatenate([high, low], axis=0), fh, preferred_element_type=f32)
+                total = both[:LANES] + both[LANES:] + jnp.dot(high, fl, preferred_element_type=f32)
+                to = pl.ds(pl.multiple_of((chunk * part + row_ref[segment * row_len + step * PAIR + p]) * LANES, LANES), LANES)
+                for i in range(2):
+                    piece = total[:, i * LANES : (i + 1) * LANES]
+                    if own:
+                        out_ref[i, to, :] = out_ref[i, to, :] - piece
+                    else:
+                        out_ref[i, to, :] = out_ref[i, to, :] + piece
+            return 0
+
+        lax.fori_loop(0, steps, product, 0)
         return 0
 
-    lax.fori_loop(0, steps, product, 0)
-
-
-def finish_kernel(parts, inner_ref, base_ref, *refs):
-    part_refs = refs[:parts]
+    lax.fori_loop(0, count, per_chunk, 0)
+
+
+def finish_kernel(parts, chunks, tiles, base_ref, *refs):
     up_ref, down_ref, res_ref, side_ref = refs[-4:]
+
+    def pick(at):
+        value = refs[at][...]
+        for c in range(1, chunks):
+            value = jnp.where(pl.program_id(0) >= c * tiles, refs[c * (parts + 1) + at][...], value)
+        return value
+
     low = base_ref[0]
     high = base_ref[1]
-    for ref in part_refs:
-        low = low - ref[0]
-        high = high - ref[1]
-    rows = (low, inner_ref[0], inner_ref[1], high)
+    for at in range(parts):
+        received = pick(at)
+        low = low - received[0]
+        high = high - received[1]
+    inner = pick(parts)
+    rows = (low, inner[0], inner[1], high)
     down_ref[...] = low
     up_ref[...] = high
     square = (LANES, LANES)
@@ -449,15 +464,13 @@
     lax.fori_loop(0, LANES // sub, body, 0, unroll=UNROLL)
 
 
-def mean_weights(mean_coef, from_left, from_right, first, moved):
+def mean_weights(mean_coef, low, high, moved):
     rows = mean_coef.shape[0]
     depth = SWEEPS
-    before = jnp.flip(from_left[4 : 4 + depth, first : first + rows].T, axis=1)
-    after = from_right[4 : 4 + depth, first : first + rows].T
-    wide = jnp.concatenate([before, mean_coef, after], axis=1)
-    low = moved(wide[rows - depth :], "sx", 1)
-    high = moved(wide[:depth], "sx", -1)
-    win = jnp.concatenate([low, wide, high], axis=0)
+    win = jnp.concatenate([low[rows - depth :], mean_coef, high[:depth]], axis=0)
+    before = moved(win[:, -depth:], "sy", 1)
+    after = moved(win[:, :depth], "sy", -1)
+    win = jnp.concatenate([before, win, after], axis=1)
     center = win[1:-1, 1:-1]
     near = (win[:-2, 1:-1], win[2:, 1:-1], win[1:-1, :-2], win[1:-1, 2:])
     near = [0.5 * (center + other) for other in near]
@@ -532,20 +545,21 @@
                 pltpu.VMEM((LANES, LANES), f32),
             ],
             compiler_params=params(),
+            cost_estimate=LITTLE,
             name="flux_edge" if halos else "flux_inner",
         )(*operands)
 
-    def couple(halves, shift, chunk, base=None):
+    def couple(halves, shift, first, count, base=None):
         own = base is not None
         operands = list(lists) + [coupling, *halves]
         specs = [smem()] * 3 + [pl.BlockSpec(memory_space=pl.ANY), whole(), whole()]
         if own:
             operands.append(base)
             specs.append(whole())
-        cfg = (terms, blocks, owners, chunks, part, shift, chunk, own)
+        cfg = (terms, blocks, owners, chunks, part, shift, first, count, own)
         return pl.pallas_call(
             functools.partial(couple_kernel, cfg),
-            out_shape=shape(2, size, LANES),
+            out_shape=shape(2, count * size, LANES),
             in_specs=specs,
             out_specs=whole(),
             scratch_shapes=[
@@ -553,91 +567,97 @@
                 pltpu.SemaphoreType.DMA((SLOTS,)),
             ],
             compiler_params=params(),
-            cost_estimate=pl.CostEstimate(
-                flops=3 * terms * modes * size * 2 * LANES,
-                bytes_accessed=terms * modes * size * 2,
-                transcendentals=0,
-            ),
+            cost_estimate=LITTLE,
             name="couple_own" if own else "couple_other",
         )(*operands)
 
     def tie(value, *others):
         return lax.optimization_barrier((value, *others))[0]
 
-    def coupled(halves, base):
-        parts = [[couple(halves, s, c) for s in range(1, owners)] for c in range(chunks)]
-        base = tie(base, *[p for ps in parts for p in ps])
-        received = [[moved(p, "mode", s + 1) for s, p in enumerate(ps)] for ps in parts]
-        own = []
+    def others(high, low):
+        received = []
         for c in range(chunks):
-            own.append(couple(halves, 0, c, base))
-            base = tie(base, own[-1])
-        return own, received
-
-    inner_high, inner_low, inner_base = fluxes((1, 2), ())
-    inner, inner_parts = coupled((inner_high, inner_low), inner_base)
+            parts = [couple((high, low), s, c, 1) for s in range(1, owners)]
+            if parts:
+                high = tie(high, *parts)
+            received.append([moved(p, "mode", s + 1) for s, p in enumerate(parts)])
+        return high, received
+
+    inner_high, inner_low, base = fluxes((1, 2), ())
+    inner_high, received = others(inner_high, inner_low)
+    inner = []
+    for c in range(chunks):
+        value = couple((inner_high, inner_low), 0, c, 1, base)
+        for part_c in received[c]:
+            value = value - part_c
+        inner.append(value)
+        base = tie(base, value)
     low, high = lax.optimization_barrier((low, high, inner[-1]))[:2]
-    for c in range(chunks):
-        for value in inner_parts[c]:
-            inner[c] = inner[c] - value
     low_in = [moved(v, "sx", 1) for v in inner]
     high_in = [moved(v, "sx", -1) for v in inner]
+    at = modes + terms + 1
+    main, corner = mean_weights(mean_coef, low[at : at + width_x], high[at : at + width_x], moved)
     edge_high, edge_low, edge_base = fluxes((0, 3), (low, high))
-    edge, edge_parts = coupled((edge_high, edge_low), edge_base)
-
-    main, corner = mean_weights(mean_coef, from_left, from_right, terms * width_x, moved)
+    edge_high, main, corner = lax.optimization_barrier((edge_high, main, corner))
+    edge_high, received = others(edge_high, edge_low)
+    edge_base, low_in[0], high_in[0] = lax.optimization_barrier((edge_base, low_in[0], high_in[0]))
+    edge = couple((edge_high, edge_low), 0, 0, chunks, edge_base)
+
     tiles = part
-    ext = 8 * tiles
-    pair = pl.BlockSpec((2, LANES, LANES), lambda k: (0, k, 0))
-    row = pl.BlockSpec((LANES, LANES), lambda k: (k, 0))
-    near = pl.BlockSpec((32, LANES), lambda k: (0, k))
-    tail = pl.BlockSpec((ext, LANES), lambda k: (size // ext, 0))
-    columns = pl.BlockSpec((32, size), lambda k: (0, 0))
+    ext = 8 * blocks
+    row_spec = pl.BlockSpec((LANES, LANES), lambda k: (k, 0))
+    pair_spec = pl.BlockSpec((2, LANES, LANES), lambda k: (0, k, 0))
     anywhere = pl.BlockSpec(memory_space=pl.ANY)
 
-    def wide(c):
-        return pl.BlockSpec((4 * LANES, LANES), lambda k: (c * tiles + k, 0))
-
-    residual = None
-    sends = []
-    for c in range(chunks):
-        operands = [inner[c], edge[c], *edge_parts[c]]
-        specs = [pair] * len(operands)
-        aliases = {}
-        if c:
-            aliases = {len(operands): 2}
-            operands.append(residual)
-            specs.append(anywhere)
-        up, down, residual, side = pl.pallas_call(
-            functools.partial(finish_kernel, len(edge_parts[c])),
-            out_shape=(shape(size + ext, LANES),) * 2 + (shape(modes * 4, LANES), shape(32, size)),
-            grid=(tiles,),
-            in_specs=specs,
-            out_specs=(row, row, wide(c), near),
-            input_output_aliases=aliases,
-            compiler_params=params(),
-            name="finish",
-        )(*operands)
-        side_left = moved(side, "sy", 1)
-        side_right = moved(side, "sy", -1)
-        up, down = pl.pallas_call(
-            functools.partial(extra_kernel, tiles),
-            out_shape=(shape(size + ext, LANES),) * 2,
-            grid=(1,),
-            in_specs=[columns] * 3 + [anywhere] * 2,
-            out_specs=(tail, tail),
-            input_output_aliases={3: 0, 4: 1},
-            compiler_params=params(),
-            name="extra",
-        )(side, side_left, side_right, up, down)
-        sends.append((up, down, side, side_left, side_right, moved(up, "sx", 1), moved(down, "sx", -1)))
+    def inner_spec(c):
+        return pl.BlockSpec((2, LANES, LANES), lambda k: (0, jnp.clip(k - c * tiles, 0, tiles - 1), 0))
+
+    up, down, residual, side = pl.pallas_call(
+        functools.partial(finish_kernel, owners - 1, chunks, tiles),
+        out_shape=(shape(modes + ext, LANES),) * 2 + (shape(modes * 4, LANES), shape(32, modes)),
+        grid=(blocks,),
+        in_specs=[pair_spec] + [inner_spec(c) for c in range(chunks) for _ in range(owners)],
+        out_specs=(
+            row_spec,
+            row_spec,
+            pl.BlockSpec((4 * LANES, LANES), lambda k: (k, 0)),
+            pl.BlockSpec((32, LANES), lambda k: (0, k)),
+        ),
+        compiler_params=params(),
+        cost_estimate=LITTLE,
+        name="finish",
+    )(edge, *[v for c in range(chunks) for v in (*received[c], inner[c])])
+    side_left = moved(side, "sy", 1)
+    side_right = moved(side, "sy", -1)
+    columns = pl.BlockSpec((32, modes), lambda k: (0, 0))
+    tail = pl.BlockSpec((ext, LANES), lambda k: (modes // ext, 0))
+    up, down = pl.pallas_call(
+        functools.partial(extra_kernel, blocks),
+        out_shape=(shape(modes + ext, LANES),) * 2,
+        grid=(1,),
+        in_specs=[columns] * 3 + [anywhere] * 2,
+        out_specs=(tail, tail),
+        input_output_aliases={3: 0, 4: 1},
+        compiler_params=params(),
+        cost_estimate=LITTLE,
+        name="extra",
+    )(side, side_left, side_right, up, down)
+    if chunks > 1:
+        up, down, *rest = lax.optimization_barrier((up, down, *low_in[1:], *high_in[1:]))
+        low_in[1:] = rest[: chunks - 1]
+        high_in[1:] = rest[chunks - 1 :]
+    low = moved(up, "sx", 1)
+    high = moved(down, "sx", -1)
 
     solution = None
     for c in range(chunks):
-        up, down, side, side_left, side_right, low, high = sends[c]
+        wide = pl.BlockSpec((4 * LANES, LANES), lambda k: (c * tiles + k, 0))
+        row = pl.BlockSpec((LANES, LANES), lambda k: (c * tiles + k, 0))
+        tail = pl.BlockSpec((8 * tiles, LANES), lambda k: (modes // (8 * tiles) + c, 0))
+        columns = pl.BlockSpec((32, size), lambda k: (0, c))
         operands = [f, inner[c], low_in[c], high_in[c], up, down, low, high, low, high]
         operands += [side, side_left, side_right, main, corner]
-        specs = [wide(c), pair, pair, pair, row, row, row, row, tail, tail, columns, columns, columns]
+        specs = [wide, pair_spec, pair_spec, pair_spec, row, row, row, row, tail, tail, columns, columns, columns]
         specs += [
             pl.BlockSpec((5, 8, LANES), lambda k: (0, 0, 0)),
             pl.BlockSpec((16, LANES), lambda k: (0, 0)),
@@ -652,7 +672,7 @@
             out_shape=shape(modes * 4, LANES),
             grid=(tiles,),
             in_specs=specs,
-            out_specs=wide(c),
+            out_specs=wide,
             input_output_aliases=aliases,
             scratch_shapes=[
                 pltpu.VMEM((10, 16, size), f32),
@@ -660,6 +680,7 @@
                 pltpu.VMEM((size, LANES), f32),
             ],
             compiler_params=params(),
+            cost_estimate=LITTLE,
             name="correct",
         )(*operands)
     full = (modes, width_x, width_y)

time: 198 us -> 177 us (0.89); the launches traced: 195 us -> 178 us
  Pallas kernels: 112 us -> 99 us
  local copies, waits for them, and re-layouts: 24.5 us -> 16.8 us
  waiting for transfers between devices: 25.8 us -> 30.9 us
    pallas_call x8 -> x7, Pallas kernels: 72.9 us -> 64.5 us  [couple(): pl.pallas_call(functools.partial(couple_kernel, cfg), out_shape=shape(2,...]
    ppermute x22 -> x18, waiting for transfers between devices: 25.8 us -> 30.9 us  [moved(): lax.ppermute(value, axis, [(i, (i + step) % devices) for i in range(devic...]
    pallas_call x2 -> x0, local copies, waits for them, and re-layouts: 2.02 us -> none  [local(): pl.pallas_call(functools.partial(pack_kernel, modes, terms), out_shape=(s...]
    pallas_call x4 -> x2, Pallas kernels: 5.71 us -> 4.19 us  [the longest x1 4.15 us: local(): pl.pallas_call(functools.partial(finish_kernel, owners - 1, chunks, tiles...]
    ppermute x22 -> x18, starting transfers between devices: 30.8 us -> 29.9 us  [moved(): lax.ppermute(value, axis, [(i, (i + step) % devices) for i in range(devic...]
    unnamed x66 -> x26, local copies, waits for them, and re-layouts: 16 us -> 16.4 us
  transfers between devices with their start and end apart: 22 -> 18, of which waited for: 4 -> 4; matrix products, arithmetic and copies ran while one was open for 4% -> 1% of each run, Pallas kernels for 53% -> 48%
where the time goes in v1:
time: 177 us; the launch traced here: 178 us
  Pallas kernels  99 us (56%)
  waiting for transfers between devices  30.9 us (17%)
  starting transfers between devices  29.9 us (17%)
  local copies, waits for them, and re-layouts  16.8 us (9%)
    pallas_call x7, Pallas kernels, couple(): pl.pallas_call(functools.partial(couple_kernel, cfg), out_shape=shape(2,...  64.5 us
    ppermute x18, waiting for transfers between devices, moved(): lax.ppermute(value, axis, [(i, (i + step) % devices) for i in range(devic...  30.9 us
    ppermute x18, starting transfers between devices, moved(): lax.ppermute(value, axis, [(i, (i + step) % devices) for i in range(devic...  29.9 us
    unnamed x26, local copies, waits for them, and re-layouts  16.4 us
    pallas_call x2, Pallas kernels, local(): pl.pallas_call(functools.partial(correct_kernel, size), out_shape=shape(m...  12.1 us
    pallas_call x2, Pallas kernels, fluxes(): pl.pallas_call(functools.partial(flux_kernel, cfg), out_shape=(halves, ha...  11.4 us
    pallas_call x1, Pallas kernels, local(): pl.pallas_call(functools.partial(list_kernel, segments, terms, blocks, pa...  5.44 us
    pallas_call x1, Pallas kernels, local(): pl.pallas_call(functools.partial(finish_kernel, owners - 1, chunks, tiles...  4.15 us
  transfers between devices with their start and end apart: 18, of which 4 were waited for; matrix products, arithmetic and copies ran while one was open for 1% of the time, Pallas kernels for 48%

profile of v1, /device:TPU:0, one launch (start us, length us, event | category | flops | bytes accessed | tf_op | source)
XLA Modules:
  0.0 178.1 jit_solution(9503508360903184736)
XLA Ops:
  5.4 2.0 %collective-permute-start.1 = (f32[8,1024]{1,0:T(8,128)S(1)}, f32[8,1024]{1,0:T(8,128)S(1)}, u32[]{:S(2)}, u32[]{:S(2)}) collective-permute-start(f32[8,1024]{1,0:T(8,128)S(1)} %get-tuple-element.42), channel_id=1, source_target_pairs={{0,3},{1,0},{2,1},{3,2},{4,7},{5,4},{6,5},{7,6},{8,11},{9,8},{10,9... | collective-permute-start | bytes 98312 | tf_op jit(solution)/shard_map/ppermute | solution.py:497
  7.4 2.3 %collective-permute-start.4 = (f32[1040,128]{1,0:T(8,128)S(1)}, f32[1040,128]{1,0:T(8,128)S(1)}, u32[]{:S(2)}, u32[]{:S(2)}) collective-permute-start(f32[1040,128]{1,0:T(8,128)S(1)} %get-tuple-element.49), channel_id=1, source_target_pairs={{0,4},{4,8},{8,12},{12,0},{1,5},{5,9},{9,13},{13,1},{2,6},{6,10},{... | collective-permute-start | bytes 1597448 | tf_op jit(solution)/shard_map/ppermute | solution.py:497
  9.7 2.0 %collective-permute-start.5 = (f32[1040,128]{1,0:T(8,128)S(1)}, f32[1040,128]{1,0:T(8,128)S(1)}, u32[]{:S(2)}, u32[]{:S(2)}) collective-permute-start(f32[1040,128]{1,0:T(8,128)S(1)} %get-tuple-element.50), channel_id=1, source_target_pairs={{0,12},{4,0},{8,4},{12,8},{1,13},{5,1},{9,5},{13,9},{2,14},{6,2},{... | collective-permute-start | bytes 1597448 | tf_op jit(solution)/shard_map/ppermute | solution.py:497
  12.6 5.4 %lists.1 = (s32[1120]{0:T(1024)S(1)}, s32[168]{0:T(256)S(1)}, s32[4]{0:T(128)S(1)}) custom-call(s32[8,16,16]{2,1,0:T(8,128)S(1)} %copy-done.11), custom_call_target="tpu_custom_call" | custom-call | tf_op jit(solution)/shard_map/lists/pallas_call | solution.py:520
  19.6 1.6 copy-done.7
  21.2 5.7 %flux_inner.1 = (bf16[8320,256]{1,0:T(8,128)(2,1)S(1)}, bf16[8320,256]{1,0:T(8,128)(2,1)S(1)}, f32[2,1024,128]{2,1,0:T(8,128)S(1)}) custom-call(f32[4096,128]{1,0:T(8,128)S(1)} %bitcast.18, f32[8,1024]{1,0:T(8,128)S(1)} %collective-permute-done.refs_1_.refs_3_, f32[8,1024]{1,0:T(8,128)S(1)} %collective-permute-done.1.refs_2_.refs_4_, ...), custom_call_target="tpu_custom_call" | custom-call | flops 1024 | bytes 1024 | tf_op jit(solution)/shard_map/flux_inner/pallas_call | solution.py:537
  26.9 8.7 %couple_other.4 = f32[2,512,128]{2,1,0:T(8,128)S(1)} custom-call(s32[1120]{0:T(1024)S(1)} %get-tuple-element.38.refs_0_, s32[168]{0:T(256)S(1)} %get-tuple-element.39.refs_1_, s32[4]{0:T(128)S(1)} %get-tuple-element.40.refs_2_, f32[8,2048,1024]{2,1,0:T(8,128)} %refs_3_.15, bf16[8320,256]{1,0:T(8,128)(2,1)S(1)} %get-tuple-element.46.refs_4_, ...), custom_call_target="tpu_custom_call" | custom-call | flops 1024 | bytes 1024 | tf_op jit(solution)/shard_map/couple_other/pallas_call | solution.py:560
  35.6 2.5 %collective-permute-start.2 = (f32[2,512,128]{2,1,0:T(8,128)S(1)}, f32[2,512,128]{2,1,0:T(8,128)S(1)}, u32[]{:S(2)}, u32[]{:S(2)}) collective-permute-start(f32[2,512,128]{2,1,0:T(8,128)S(1)} %couple_other.4), channel_id=1, source_target_pairs={{0,16},{16,0},{1,17},{17,1},{2,18},{18,2},{3,19},{19,3},{4,20},{20... | collective-permute-start | bytes 1572872 | tf_op jit(solution)/shard_map/ppermute | solution.py:497
  38.1 8.6 %couple_other.5 = f32[2,512,128]{2,1,0:T(8,128)S(1)} custom-call(s32[1120]{0:T(1024)S(1)} %get-tuple-element.38.refs_0_, s32[168]{0:T(256)S(1)} %get-tuple-element.39.refs_1_, s32[4]{0:T(128)S(1)} %get-tuple-element.40.refs_2_, f32[8,2048,1024]{2,1,0:T(8,128)} %refs_3_.15, bf16[8320,256]{1,0:T(8,128)(2,1)S(1)} %get-tuple-element.46.refs_4_, ...), custom_call_target="tpu_custom_call" | custom-call | flops 1024 | bytes 1024 | tf_op jit(solution)/shard_map/couple_other/pallas_call | solution.py:560
  47.0 7.8 %couple_own.3 = f32[2,512,128]{2,1,0:T(8,128)S(1)} custom-call(s32[1120]{0:T(1024)S(1)} %get-tuple-element.38.refs_0_, s32[168]{0:T(256)S(1)} %get-tuple-element.39.refs_1_, s32[4]{0:T(128)S(1)} %get-tuple-element.40.refs_2_, f32[8,2048,1024]{2,1,0:T(8,128)} %refs_3_.15, bf16[8320,256]{1,0:T(8,128)(2,1)S(1)} %get-tuple-element.46.refs_4_, ...), custom_call_target="tpu_custom_call" | custom-call | flops 1024 | bytes 1024 | tf_op jit(solution)/shard_map/couple_own/pallas_call | solution.py:560
  55.0 7.9 %couple_own.4 = f32[2,512,128]{2,1,0:T(8,128)S(1)} custom-call(s32[1120]{0:T(1024)S(1)} %get-tuple-element.38.refs_0_, s32[168]{0:T(256)S(1)} %get-tuple-element.39.refs_1_, s32[4]{0:T(128)S(1)} %get-tuple-element.40.refs_2_, f32[8,2048,1024]{2,1,0:T(8,128)} %refs_3_.15, bf16[8320,256]{1,0:T(8,128)(2,1)S(1)} %get-tuple-element.46.refs_4_, ...), custom_call_target="tpu_custom_call" | custom-call | flops 1024 | bytes 1024 | tf_op jit(solution)/shard_map/couple_own/pallas_call | solution.py:560
  63.1 1.7 collective-permute-start.7
  64.8 3.8 %collective-permute-start.9 = (f32[2,512,128]{2,1,0:T(8,128)S(1)}, f32[2,512,128]{2,1,0:T(8,128)}, u32[]{:S(2)}, u32[]{:S(2)}) collective-permute-start(f32[2,512,128]{2,1,0:T(8,128)S(1)} %sub.6.refs_1_.inner_ref), channel_id=1, source_target_pairs={{0,12},{4,0},{8,4},{12,8},{1,13},{5,1},{9,5},{13,9},{2,14},{6,2},{... | collective-permute-start | bytes 1572872 | tf_op jit(solution)/shard_map/ppermute | solution.py:497
  68.6 5.7 %flux_edge.1 = (bf16[8320,256]{1,0:T(8,128)(2,1)S(1)}, bf16[8320,256]{1,0:T(8,128)(2,1)S(1)}, f32[2,1024,128]{2,1,0:T(8,128)S(1)}) custom-call(f32[4096,128]{1,0:T(8,128)S(1)} %bitcast.19, f32[1040,128]{1,0:T(8,128)S(1)} %collective-permute-done.4.refs_1_, f32[1040,128]{1,0:T(8,128)S(1)} %collective-permute-done.5.refs_2_, ...), custom_call_target="tpu_custom_call" | custom-call | flops 1024 | bytes 1024 | tf_op jit(solution)/shard_map/flux_edge/pallas_call | solution.py:537
  74.3 2.0 %copy-done.3 = bf16[8320,256]{1,0:T(8,128)(2,1)} copy-done((bf16[8320,256]{1,0:T(8,128)(2,1)}, bf16[8320,256]{1,0:T(8,128)(2,1)S(1)}, u32[]{:S(2)}) %copy-start.3) | copy-done | bytes 4259864
  76.3 2.0 %copy-done.5 = bf16[8320,256]{1,0:T(8,128)(2,1)} copy-done((bf16[8320,256]{1,0:T(8,128)(2,1)}, bf16[8320,256]{1,0:T(8,128)(2,1)S(1)}, u32[]{:S(2)}) %copy-start.5) | copy-done | bytes 4259864
  80.2 2.2 %copy-done.4 = bf16[8320,256]{1,0:T(8,128)(2,1)S(1)} copy-done((bf16[8320,256]{1,0:T(8,128)(2,1)S(1)}, bf16[8320,256]{1,0:T(8,128)(2,1)}, u32[]{:S(2)}) %copy-start.4) | copy-done | bytes 4259864
  82.4 2.2 %copy-done.6 = bf16[8320,256]{1,0:T(8,128)(2,1)S(1)} copy-done((bf16[8320,256]{1,0:T(8,128)(2,1)S(1)}, bf16[8320,256]{1,0:T(8,128)(2,1)}, u32[]{:S(2)}) %copy-start.6) | copy-done | bytes 4259864
  84.6 8.5 %couple_other.6 = f32[2,512,128]{2,1,0:T(8,128)S(1)} custom-call(s32[1120]{0:T(1024)S(1)} %get-tuple-element.38.refs_0_, s32[168]{0:T(256)S(1)} %get-tuple-element.39.refs_1_, s32[4]{0:T(128)S(1)} %get-tuple-element.40.refs_2_, f32[8,2048,1024]{2,1,0:T(8,128)} %refs_3_.15, bf16[8320,256]{1,0:T(8,128)(2,1)S(1)} %copy-done.4, bf16[8320,256]{1,0:T(8,128)(2,1)S(1)} %copy-done.6), custom_call_target="tpu_custom_call" | custom-call | flops 1024 | bytes 1024 | tf_op jit(solution)/shard_map/couple_other/pallas_call | solution.py:560
  93.1 8.4 %couple_other.7 = f32[2,512,128]{2,1,0:T(8,128)S(1)} custom-call(s32[1120]{0:T(1024)S(1)} %get-tuple-element.38.refs_0_, s32[168]{0:T(256)S(1)} %get-tuple-element.39.refs_1_, s32[4]{0:T(128)S(1)} %get-tuple-element.40.refs_2_, f32[8,2048,1024]{2,1,0:T(8,128)} %refs_3_.15, bf16[8320,256]{1,0:T(8,128)(2,1)S(1)} %copy-done.4, bf16[8320,256]{1,0:T(8,128)(2,1)S(1)} %copy-done.6), custom_call_target="tpu_custom_call" | custom-call | flops 1024 | bytes 1024 | tf_op jit(solution)/shard_map/couple_other/pallas_call | solution.py:560
  101.5 5.2 %collective-permute-start.11 = (f32[2,512,128]{2,1,0:T(8,128)S(1)}, f32[2,512,128]{2,1,0:T(8,128)S(1)}, u32[]{:S(2)}, u32[]{:S(2)}) collective-permute-start(f32[2,512,128]{2,1,0:T(8,128)S(1)} %couple_other.7), channel_id=1, source_target_pairs={{0,16},{16,0},{1,17},{17,1},{2,18},{18,2},{3,19},{19,3},{4,20},{20... | collective-permute-start | bytes 1572872 | tf_op jit(solution)/shard_map/ppermute | solution.py:497
  106.7 3.8 %collective-permute-start.15 = (f32[2,512,128]{2,1,0:T(8,128)S(1)}, f32[2,512,128]{2,1,0:T(8,128)S(1)}, u32[]{:S(2)}, u32[]{:S(2)}) collective-permute-start(f32[2,512,128]{2,1,0:T(8,128)S(1)} %sub.7.refs_3_.inner_ref), channel_id=1, source_target_pairs={{0,12},{4,0},{8,4},{12,8},{1,13},{5,1},{9,5},{13,9},{2,14},{6,2},{... | collective-permute-start | bytes 1572872 | tf_op jit(solution)/shard_map/ppermute | solution.py:497
  110.6 14.7 %couple_own.5.base_ref = f32[2,1024,128]{2,1,0:T(8,128)S(1)} custom-call(s32[1120]{0:T(1024)S(1)} %get-tuple-element.38.refs_0_, s32[168]{0:T(256)S(1)} %get-tuple-element.39.refs_1_, s32[4]{0:T(128)S(1)} %get-tuple-element.40.refs_2_, f32[8,2048,1024]{2,1,0:T(8,128)} %refs_3_.15, bf16[8320,256]{1,0:T(8,128)(2,1)S(1)} %copy-done.4, ...), custom_call_target="tpu_custom_call" | custom-call | flops 1024 | bytes 1024 | tf_op jit(solution)/shard_map/couple_own/pallas_call | solution.py:560
  125.3 4.3 %collective-permute-done.10.refs_0_ = f32[2,512,128]{2,1,0:T(8,128)S(1)} collective-permute-done((f32[2,512,128]{2,1,0:T(8,128)S(1)}, f32[2,512,128]{2,1,0:T(8,128)S(1)}, u32[]{:S(2)}, u32[]{:S(2)}) %collective-permute-start.10) | collective-permute-done | bytes 524320 | tf_op jit(solution)/shard_map/ppermute | solution.py:497
  129.6 4.1 %finish.1 = (f32[1088,128]{1,0:T(8,128)S(1)}, f32[1088,128]{1,0:T(8,128)S(1)}, f32[4096,128]{1,0:T(8,128)}, f32[32,1024]{1,0:T(8,128)S(1)}) custom-call(f32[2,1024,128]{2,1,0:T(8,128)S(1)} %couple_own.5.base_ref, f32[2,512,128]{2,1,0:T(8,128)S(1)} %collective-permute-done.10.refs_0_, f32[2,512,128]{2,1,0:T(8,128)S(1)} %sub.6.refs_1_.inner_ref, ...), custom_call_target="tpu_custom_call" | custom-call | flops 1024 | bytes 1024 | tf_op jit(solution)/shard_map/finish/pallas_call | solution.py:615
  133.7 1.7 collective-permute-start.13
  135.4 3.3 %collective-permute-done.12.left_ref = f32[32,1024]{1,0:T(8,128)S(1)} collective-permute-done((f32[32,1024]{1,0:T(8,128)S(1)}, f32[32,1024]{1,0:T(8,128)S(1)}, u32[]{:S(2)}, u32[]{:S(2)}) %collective-permute-start.12) | collective-permute-done | bytes 131104 | tf_op jit(solution)/shard_map/ppermute | solution.py:497
  138.9 3.8 %collective-permute-start.17 = (f32[1088,128]{1,0:T(8,128)S(1)}, f32[1088,128]{1,0:T(8,128)S(1)}, u32[]{:S(2)}, u32[]{:S(2)}) collective-permute-start(f32[1088,128]{1,0:T(8,128)S(1)} %get-tuple-element.68.down_ref), channel_id=1, source_target_pairs={{0,12},{4,0},{8,4},{12,8},{1,13},{5,1},{9,5},{13,9},{2,14},{6,2},{... | collective-permute-start | bytes 1671176 | tf_op jit(solution)/shard_map/ppermute | solution.py:497
  142.7 13.4 %collective-permute-done.16.low_ref.low_x_ref = f32[1088,128]{1,0:T(8,128)S(1)} collective-permute-done((f32[1088,128]{1,0:T(8,128)S(1)}, f32[1088,128]{1,0:T(8,128)S(1)}, u32[]{:S(2)}, u32[]{:S(2)}) %collective-permute-start.16) | collective-permute-done | bytes 557088 | tf_op jit(solution)/shard_map/ppermute | solution.py:497
  156.1 9.9 %collective-permute-done.17.high_ref.high_x_ref = f32[1088,128]{1,0:T(8,128)S(1)} collective-permute-done((f32[1088,128]{1,0:T(8,128)S(1)}, f32[1088,128]{1,0:T(8,128)S(1)}, u32[]{:S(2)}, u32[]{:S(2)}) %collective-permute-start.17) | collective-permute-done | bytes 557088 | tf_op jit(solution)/shard_map/ppermute | solution.py:497
  166.0 6.5 %correct.2.refs_0_ = f32[4096,128]{1,0:T(8,128)} custom-call(f32[4096,128]{1,0:T(8,128)S(1)} %bitcast.20, f32[2,512,128]{2,1,0:T(8,128)S(1)} %sub.6.refs_1_.inner_ref, f32[2,512,128]{2,1,0:T(8,128)} %collective-permute-done.8.low_in_ref, f32[2,512,128]{2,1,0:T(8,128)} %collective-permute-done.9.high_in_ref, f32[1088,128]{1,0:T(8,128)S(1)} %get-tuple-element.67.up_ref, ...), custom_call_target="tpu_custom_call" | custom-call | flops 1024 | bytes 1024 | tf_op jit(solution)/shard_map/correct/pallas_call | solution.py:670
  172.5 5.7 %correct.3 = f32[4096,128]{1,0:T(8,128)} custom-call(f32[4096,128]{1,0:T(8,128)S(1)} %bitcast.21, f32[2,512,128]{2,1,0:T(8,128)S(1)} %sub.7.refs_3_.inner_ref, f32[2,512,128]{2,1,0:T(8,128)S(1)} %collective-permute-done.14.low_in_ref, f32[2,512,128]{2,1,0:T(8,128)S(1)} %collective-permute-done.15.high_in_ref, ...), custom_call_target="tpu_custom_call", output_to_operand_aliasing={{}: (15, {})} | custom-call | flops 1024 | bytes 1024 | tf_op jit(solution)/shard_map/correct/pallas_call | solution.py:670
  (64 shorter events, 9.7 us)
Async XLA Ops:
  0.6 1.6 copy-start
  2.2 0.7 copy-start.10
  2.9 0.7 copy-start.12
  4.9 13.1 %collective-permute-start = (f32[8,1024]{1,0:T(8,128)S(1)}, f32[8,1024]{1,0:T(8,128)S(1)}, u32[]{:S(2)}, u32[]{:S(2)}) collective-permute-start(f32[8,1024]{1,0:T(8,128)S(1)} %get-tuple-element.41), channel_id=1, source_target_pairs={{0,1},{1,2},{2,3},{3,0},{4,5},{5,6},{6,7},{7,4},{8,9},{9,10},{10,1... | collective-permute-start | bytes 98312 | tf_op jit(solution)/shard_map/ppermute | solution.py:497
  5.4 12.7 %collective-permute-start.1 = (f32[8,1024]{1,0:T(8,128)S(1)}, f32[8,1024]{1,0:T(8,128)S(1)}, u32[]{:S(2)}, u32[]{:S(2)}) collective-permute-start(f32[8,1024]{1,0:T(8,128)S(1)} %get-tuple-element.42), channel_id=1, source_target_pairs={{0,3},{1,0},{2,1},{3,2},{4,7},{5,4},{6,5},{7,6},{8,11},{9,8},{10,9... | collective-permute-start | bytes 98312 | tf_op jit(solution)/shard_map/ppermute | solution.py:497
  7.4 55.5 %collective-permute-start.4 = (f32[1040,128]{1,0:T(8,128)S(1)}, f32[1040,128]{1,0:T(8,128)S(1)}, u32[]{:S(2)}, u32[]{:S(2)}) collective-permute-start(f32[1040,128]{1,0:T(8,128)S(1)} %get-tuple-element.49), channel_id=1, source_target_pairs={{0,4},{4,8},{8,12},{12,0},{1,5},{5,9},{9,13},{13,1},{2,6},{6,10},{... | collective-permute-start | bytes 1597448 | tf_op jit(solution)/shard_map/ppermute | solution.py:497
  9.7 53.2 %collective-permute-start.5 = (f32[1040,128]{1,0:T(8,128)S(1)}, f32[1040,128]{1,0:T(8,128)S(1)}, u32[]{:S(2)}, u32[]{:S(2)}) collective-permute-start(f32[1040,128]{1,0:T(8,128)S(1)} %get-tuple-element.50), channel_id=1, source_target_pairs={{0,12},{4,0},{8,4},{12,8},{1,13},{5,1},{9,5},{13,9},{2,14},{6,2},{... | collective-permute-start | bytes 1597448 | tf_op jit(solution)/shard_map/ppermute | solution.py:497
  11.7 0.8 copy-start.11
  18.0 1.6 copy-start.1
  19.6 1.6 copy-start.7
  35.6 19.2 %collective-permute-start.2 = (f32[2,512,128]{2,1,0:T(8,128)S(1)}, f32[2,512,128]{2,1,0:T(8,128)S(1)}, u32[]{:S(2)}, u32[]{:S(2)}) collective-permute-start(f32[2,512,128]{2,1,0:T(8,128)S(1)} %couple_other.4), channel_id=1, source_target_pairs={{0,16},{16,0},{1,17},{17,1},{2,18},{18,2},{3,19},{19,3},{4,20},{20... | collective-permute-start | bytes 1572872 | tf_op jit(solution)/shard_map/ppermute | solution.py:497
  46.8 16.1 %collective-permute-start.3 = (f32[2,512,128]{2,1,0:T(8,128)S(1)}, f32[2,512,128]{2,1,0:T(8,128)S(1)}, u32[]{:S(2)}, u32[]{:S(2)}) collective-permute-start(f32[2,512,128]{2,1,0:T(8,128)S(1)} %couple_other.5), channel_id=1, source_target_pairs={{0,16},{16,0},{1,17},{17,1},{2,18},{18,2},{3,19},{19,3},{4,20},{20... | collective-permute-start | bytes 1572872 | tf_op jit(solution)/shard_map/ppermute | solution.py:497
  54.9 13.7 %copy-start.2 = (f32[1024,4,128]{2,1,0:T(4,128)S(1)}, f32[1024,4,128]{2,1,0:T(4,128)}, u32[]{:S(2)}) copy-start(f32[1024,4,128]{2,1,0:T(4,128)} %param.6) | copy-start | bytes 6291460
  54.9 51.8 %collective-permute-start.8 = (f32[2,512,128]{2,1,0:T(8,128)S(1)}, f32[2,512,128]{2,1,0:T(8,128)}, u32[]{:S(2)}, u32[]{:S(2)}) collective-permute-start(f32[2,512,128]{2,1,0:T(8,128)S(1)} %sub.6.refs_1_.inner_ref), channel_id=1, source_target_pairs={{0,4},{4,8},{8,12},{12,0},{1,5},{5,9},{9,13},{13,1},{2,6},{6,10},{... | collective-permute-start | bytes 1572872 | tf_op jit(solution)/shard_map/ppermute | solution.py:497
  63.1 16.3 %collective-permute-start.6 = (f32[10,3]{1,0:T(8,128)S(1)}, f32[10,3]{1,0:T(8,128)S(1)}, u32[]{:S(2)}, u32[]{:S(2)}) collective-permute-start(f32[10,3]{1,0:T(8,128)S(1)} %get-tuple-element.76), channel_id=1, source_target_pairs={{0,1},{1,2},{2,3},{3,0},{4,5},{5,6},{6,7},{7,4},{8,9},{9,10},{10,1... | collective-permute-start | bytes 368 | tf_op jit(solution)/shard_map/ppermute | solution.py:497
  63.1 16.3 %collective-permute-start.7 = (f32[10,3]{1,0:T(8,128)S(1)}, f32[10,3]{1,0:T(8,128)S(1)}, u32[]{:S(2)}, u32[]{:S(2)}) collective-permute-start(f32[10,3]{1,0:T(8,128)S(1)} %get-tuple-element.77), channel_id=1, source_target_pairs={{0,3},{1,0},{2,1},{3,2},{4,7},{5,4},{6,5},{7,6},{8,11},{9,8},{10,9... | collective-permute-start | bytes 368 | tf_op jit(solution)/shard_map/ppermute | solution.py:497
  64.8 45.7 %collective-permute-start.9 = (f32[2,512,128]{2,1,0:T(8,128)S(1)}, f32[2,512,128]{2,1,0:T(8,128)}, u32[]{:S(2)}, u32[]{:S(2)}) collective-permute-start(f32[2,512,128]{2,1,0:T(8,128)S(1)} %sub.6.refs_1_.inner_ref), channel_id=1, source_target_pairs={{0,12},{4,0},{8,4},{12,8},{1,13},{5,1},{9,5},{13,9},{2,14},{6,2},{... | collective-permute-start | bytes 1572872 | tf_op jit(solution)/shard_map/ppermute | solution.py:497
  74.3 2.0 %copy-start.3 = (bf16[8320,256]{1,0:T(8,128)(2,1)}, bf16[8320,256]{1,0:T(8,128)(2,1)S(1)}, u32[]{:S(2)}) copy-start(bf16[8320,256]{1,0:T(8,128)(2,1)S(1)} %get-tuple-element.57.refs_4_) | copy-start | bytes 12779524
  76.3 2.0 %copy-start.5 = (bf16[8320,256]{1,0:T(8,128)(2,1)}, bf16[8320,256]{1,0:T(8,128)(2,1)S(1)}, u32[]{:S(2)}) copy-start(bf16[8320,256]{1,0:T(8,128)(2,1)S(1)} %get-tuple-element.55.refs_5_) | copy-start | bytes 12779524
  78.4 1.0 copy-start.8
  80.2 2.2 %copy-start.4 = (bf16[8320,256]{1,0:T(8,128)(2,1)S(1)}, bf16[8320,256]{1,0:T(8,128)(2,1)}, u32[]{:S(2)}) copy-start(bf16[8320,256]{1,0:T(8,128)(2,1)} %copy-done.3) | copy-start | bytes 12779524
  82.4 2.2 %copy-start.6 = (bf16[8320,256]{1,0:T(8,128)(2,1)S(1)}, bf16[8320,256]{1,0:T(8,128)(2,1)}, u32[]{:S(2)}) copy-start(bf16[8320,256]{1,0:T(8,128)(2,1)} %copy-done.5) | copy-start | bytes 12779524
  93.1 17.5 %copy-start.9 = (f32[2,1024,128]{2,1,0:T(8,128)S(1)}, f32[2,1024,128]{2,1,0:T(8,128)}, u32[]{:S(2)}) copy-start(f32[2,1024,128]{2,1,0:T(8,128)} %copy-done.8) | copy-start | bytes 3145732
  101.5 23.8 %collective-permute-start.11 = (f32[2,512,128]{2,1,0:T(8,128)S(1)}, f32[2,512,128]{2,1,0:T(8,128)S(1)}, u32[]{:S(2)}, u32[]{:S(2)}) collective-permute-start(f32[2,512,128]{2,1,0:T(8,128)S(1)} %couple_other.7), channel_id=1, source_target_pairs={{0,16},{16,0},{1,17},{17,1},{2,18},{18,2},{3,19},{19,3},{4,20},{20... | collective-permute-start | bytes 1572872 | tf_op jit(solution)/shard_map/ppermute | solution.py:497
  106.7 22.9 %collective-permute-start.10 = (f32[2,512,128]{2,1,0:T(8,128)S(1)}, f32[2,512,128]{2,1,0:T(8,128)S(1)}, u32[]{:S(2)}, u32[]{:S(2)}) collective-permute-start(f32[2,512,128]{2,1,0:T(8,128)S(1)} %couple_other.6), channel_id=1, source_target_pairs={{0,16},{16,0},{1,17},{17,1},{2,18},{18,2},{3,19},{19,3},{4,20},{20... | collective-permute-start | bytes 1572872 | tf_op jit(solution)/shard_map/ppermute | solution.py:497
  106.7 32.1 %collective-permute-start.14 = (f32[2,512,128]{2,1,0:T(8,128)S(1)}, f32[2,512,128]{2,1,0:T(8,128)S(1)}, u32[]{:S(2)}, u32[]{:S(2)}) collective-permute-start(f32[2,512,128]{2,1,0:T(8,128)S(1)} %sub.7.refs_3_.inner_ref), channel_id=1, source_target_pairs={{0,4},{4,8},{8,12},{12,0},{1,5},{5,9},{9,13},{13,1},{2,6},{6,10},{... | collective-permute-start | bytes 1572872 | tf_op jit(solution)/shard_map/ppermute | solution.py:497
  106.7 32.1 %collective-permute-start.15 = (f32[2,512,128]{2,1,0:T(8,128)S(1)}, f32[2,512,128]{2,1,0:T(8,128)S(1)}, u32[]{:S(2)}, u32[]{:S(2)}) collective-permute-start(f32[2,512,128]{2,1,0:T(8,128)S(1)} %sub.7.refs_3_.inner_ref), channel_id=1, source_target_pairs={{0,12},{4,0},{8,4},{12,8},{1,13},{5,1},{9,5},{13,9},{2,14},{6,2},{... | collective-permute-start | bytes 1572872 | tf_op jit(solution)/shard_map/ppermute | solution.py:497
  133.7 5.0 %collective-permute-start.12 = (f32[32,1024]{1,0:T(8,128)S(1)}, f32[32,1024]{1,0:T(8,128)S(1)}, u32[]{:S(2)}, u32[]{:S(2)}) collective-permute-start(f32[32,1024]{1,0:T(8,128)S(1)} %get-tuple-element.60.side_ref), channel_id=1, source_target_pairs={{0,1},{1,2},{2,3},{3,0},{4,5},{5,6},{6,7},{7,4},{8,9},{9,10},{10,1... | collective-permute-start | bytes 393224 | tf_op jit(solution)/shard_map/ppermute | solution.py:497
  133.7 5.0 %collective-permute-start.13 = (f32[32,1024]{1,0:T(8,128)S(1)}, f32[32,1024]{1,0:T(8,128)S(1)}, u32[]{:S(2)}, u32[]{:S(2)}) collective-permute-start(f32[32,1024]{1,0:T(8,128)S(1)} %get-tuple-element.60.side_ref), channel_id=1, source_target_pairs={{0,3},{1,0},{2,1},{3,2},{4,7},{5,4},{6,5},{7,6},{8,11},{9,8},{10,9... | collective-permute-start | bytes 393224 | tf_op jit(solution)/shard_map/ppermute | solution.py:497
  138.8 17.3 %collective-permute-start.16 = (f32[1088,128]{1,0:T(8,128)S(1)}, f32[1088,128]{1,0:T(8,128)S(1)}, u32[]{:S(2)}, u32[]{:S(2)}) collective-permute-start(f32[1088,128]{1,0:T(8,128)S(1)} %get-tuple-element.67.up_ref), channel_id=1, source_target_pairs={{0,4},{4,8},{8,12},{12,0},{1,5},{5,9},{9,13},{13,1},{2,6},{6,10},{... | collective-permute-start | bytes 1671176 | tf_op jit(solution)/shard_map/ppermute | solution.py:497
  138.9 27.1 %collective-permute-start.17 = (f32[1088,128]{1,0:T(8,128)S(1)}, f32[1088,128]{1,0:T(8,128)S(1)}, u32[]{:S(2)}, u32[]{:S(2)}) collective-permute-start(f32[1088,128]{1,0:T(8,128)S(1)} %get-tuple-element.68.down_ref), channel_id=1, source_target_pairs={{0,12},{4,0},{8,4},{12,8},{1,13},{5,1},{9,5},{13,9},{2,14},{6,2},{... | collective-permute-start | bytes 1671176 | tf_op jit(solution)/shard_map/ppermute | solution.py:497

commit v2 on v1

--- a/solution.py
+++ b/solution.py
@@ -21,7 +21,7 @@
 PAD = 16
 SUB = 32
 UNROLL = 4
-VMEM_LIMIT = 24 * 1024 * 1024
+VMEM_LIMIT = 17 * 1024 * 1024
 
 LITTLE = pl.CostEstimate(flops=1024, bytes_accessed=1024, transcendentals=0)
 
@@ -108,17 +108,19 @@
     return groups * GROUP + GROUP, groups + most
 
 
-def list_kernel(segments, terms, blocks, part, mask_ref, list_ref, row_ref, count_ref):
+def list_kernel(segments, total, terms, blocks, part, mask_ref, list_ref, row_ref, count_ref):
     length, rows = list_sizes(terms, blocks, part)
     most = -(-terms * blocks // GROUP)
     none = terms * blocks
+    square = total * total
     me = lax.axis_index("mode")
 
     def per_segment(o, _):
         def per_row(a, base):
             count = base
+            place = (o * part + a) * total + me * blocks
             for t in range(terms):
-                found = [mask_ref[t, o * part + a, me * blocks + b] for b in range(blocks)]
+                found = [mask_ref[place + t * square + b] for b in range(blocks)]
                 for b in range(blocks):
                     list_ref[o * length + count] = t * blocks + b
                     count = count + found[b]
@@ -129,12 +131,12 @@
                 row_ref[o * rows + group + k] = a
             return base + (count - base + GROUP - 1) // GROUP * GROUP
 
-        total = lax.fori_loop(0, part, per_row, 0)
+        filled = lax.fori_loop(0, part, per_row, 0)
         for k in range((PAIR - 1) * GROUP):
-            list_ref[o * length + total + k] = none
+            list_ref[o * length + filled + k] = none
         for k in range(PAIR - 1):
-            row_ref[o * rows + total // GROUP + k] = 0
-        count_ref[o] = (total // GROUP + PAIR - 1) // PAIR
+            row_ref[o * rows + filled // GROUP + k] = 0
+        count_ref[o] = (filled // GROUP + PAIR - 1) // PAIR
         return 0
 
     lax.fori_loop(0, segments, per_segment, 0)
@@ -318,23 +320,14 @@
     lax.fori_loop(0, count, per_chunk, 0)
 
 
-def finish_kernel(parts, chunks, tiles, base_ref, *refs):
+def finish_kernel(parts, inner_ref, base_ref, *refs):
     up_ref, down_ref, res_ref, side_ref = refs[-4:]
-
-    def pick(at):
-        value = refs[at][...]
-        for c in range(1, chunks):
-            value = jnp.where(pl.program_id(0) >= c * tiles, refs[c * (parts + 1) + at][...], value)
-        return value
-
     low = base_ref[0]
     high = base_ref[1]
-    for at in range(parts):
-        received = pick(at)
-        low = low - received[0]
-        high = high - received[1]
-    inner = pick(parts)
-    rows = (low, inner[0], inner[1], high)
+    for ref in refs[:parts]:
+        low = low - ref[0]
+        high = high - ref[1]
+    rows = (low, inner_ref[0], inner_ref[1], high)
     down_ref[...] = low
     up_ref[...] = high
     square = (LANES, LANES)
@@ -518,7 +511,7 @@
     segments = owners * chunks
     length, row_len = list_sizes(terms, blocks, part)
     lists = pl.pallas_call(
-        functools.partial(list_kernel, segments, terms, blocks, part),
+        functools.partial(list_kernel, segments, block_mask.shape[1], terms, blocks, part),
         out_shape=(
             jax.ShapeDtypeStruct((segments * length,), jnp.int32),
             jax.ShapeDtypeStruct((segments * row_len,), jnp.int32),
@@ -528,7 +521,7 @@
         out_specs=(smem(),) * 3,
         compiler_params=params(),
         name="lists",
-    )(block_mask)
+    )(block_mask.reshape(-1))
 
     def fluxes(rows, halos):
         operands = [f, *halos, from_left, from_right, mean_coef, term, rs]
@@ -597,67 +590,79 @@
     high_in = [moved(v, "sx", -1) for v in inner]
     at = modes + terms + 1
     main, corner = mean_weights(mean_coef, low[at : at + width_x], high[at : at + width_x], moved)
+    low, high, main, corner = lax.optimization_barrier((low, high, main, corner))
     edge_high, edge_low, edge_base = fluxes((0, 3), (low, high))
-    edge_high, main, corner = lax.optimization_barrier((edge_high, main, corner))
     edge_high, received = others(edge_high, edge_low)
     edge_base, low_in[0], high_in[0] = lax.optimization_barrier((edge_base, low_in[0], high_in[0]))
-    edge = couple((edge_high, edge_low), 0, 0, chunks, edge_base)
 
     tiles = part
-    ext = 8 * blocks
-    row_spec = pl.BlockSpec((LANES, LANES), lambda k: (k, 0))
-    pair_spec = pl.BlockSpec((2, LANES, LANES), lambda k: (0, k, 0))
+    ext = 8 * tiles
+    pair = pl.BlockSpec((2, LANES, LANES), lambda k: (0, k, 0))
+    row = pl.BlockSpec((LANES, LANES), lambda k: (k, 0))
+    near = pl.BlockSpec((32, LANES), lambda k: (0, k))
+    tail = pl.BlockSpec((ext, LANES), lambda k: (size // ext, 0))
+    columns = pl.BlockSpec((32, size), lambda k: (0, 0))
     anywhere = pl.BlockSpec(memory_space=pl.ANY)
 
-    def inner_spec(c):
-        return pl.BlockSpec((2, LANES, LANES), lambda k: (0, jnp.clip(k - c * tiles, 0, tiles - 1), 0))
-
-    up, down, residual, side = pl.pallas_call(
-        functools.partial(finish_kernel, owners - 1, chunks, tiles),
-        out_shape=(shape(modes + ext, LANES),) * 2 + (shape(modes * 4, LANES), shape(32, modes)),
-        grid=(blocks,),
-        in_specs=[pair_spec] + [inner_spec(c) for c in range(chunks) for _ in range(owners)],
-        out_specs=(
-            row_spec,
-            row_spec,
-            pl.BlockSpec((4 * LANES, LANES), lambda k: (k, 0)),
-            pl.BlockSpec((32, LANES), lambda k: (0, k)),
-        ),
-        compiler_params=params(),
-        cost_estimate=LITTLE,
-        name="finish",
-    )(edge, *[v for c in range(chunks) for v in (*received[c], inner[c])])
-    side_left = moved(side, "sy", 1)
-    side_right = moved(side, "sy", -1)
-    columns = pl.BlockSpec((32, modes), lambda k: (0, 0))
-    tail = pl.BlockSpec((ext, LANES), lambda k: (modes // ext, 0))
-    up, down = pl.pallas_call(
-        functools.partial(extra_kernel, blocks),
-        out_shape=(shape(modes + ext, LANES),) * 2,
-        grid=(1,),
-        in_specs=[columns] * 3 + [anywhere] * 2,
-        out_specs=(tail, tail),
-        input_output_aliases={3: 0, 4: 1},
-        compiler_params=params(),
-        cost_estimate=LITTLE,
-        name="extra",
-    )(side, side_left, side_right, up, down)
-    if chunks > 1:
-        up, down, *rest = lax.optimization_barrier((up, down, *low_in[1:], *high_in[1:]))
-        low_in[1:] = rest[: chunks - 1]
-        high_in[1:] = rest[chunks - 1 :]
-    low = moved(up, "sx", 1)
-    high = moved(down, "sx", -1)
+    def wide(c):
+        return pl.BlockSpec((4 * LANES, LANES), lambda k: (c * tiles + k, 0))
+
+    def ready(chunk):
+        up, down, side, side_left, side_right = chunk
+        up, down = pl.pallas_call(
+            functools.partial(extra_kernel, tiles),
+            out_shape=(shape(size + ext, LANES),) * 2,
+            grid=(1,),
+            in_specs=[columns] * 3 + [anywhere] * 2,
+            out_specs=(tail, tail),
+            input_output_aliases={3: 0, 4: 1},
+            compiler_params=params(),
+            cost_estimate=LITTLE,
+            name="extra",
+        )(side, side_left, side_right, up, down)
+        return up, down, side, side_left, side_right
+
+    residual = None
+    sends = []
+    waiting = None
+    for c in range(chunks):
+        edge = couple((edge_high, edge_low), 0, c, 1, edge_base)
+        if c:
+            up, down, side, side_left, side_right = waiting
+            waiting = ready((up, down, side, tie(side_left, edge), side_right))
+            up, down, edge, *rest = lax.optimization_barrier((*waiting[:2], edge, *low_in[c:], *high_in[c:]))
+            low_in[c:] = rest[: chunks - c]
+            high_in[c:] = rest[chunks - c :]
+            sends.append((up, down, *waiting[2:], moved(up, "sx", 1), moved(down, "sx", -1)))
+        operands = [inner[c], edge, *received[c]]
+        specs = [pair] * len(operands)
+        aliases = {}
+        if c:
+            aliases = {len(operands): 2}
+            operands.append(residual)
+            specs.append(anywhere)
+        up, down, residual, side = pl.pallas_call(
+            functools.partial(finish_kernel, len(received[c])),
+            out_shape=(shape(size + ext, LANES),) * 2 + (shape(modes * 4, LANES), shape(32, size)),
+            grid=(tiles,),
+            in_specs=specs,
+            out_specs=(row, row, wide(c), near),
+            input_output_aliases=aliases,
+            compiler_params=params(),
+            cost_estimate=LITTLE,
+            name="finish",
+        )(*operands)
+        edge_base = tie(edge_base, side)
+        waiting = (up, down, side, moved(side, "sy", 1), moved(side, "sy", -1))
+    up, down, *rest = ready(waiting)
+    sends.append((up, down, *rest, moved(up, "sx", 1), moved(down, "sx", -1)))
 
     solution = None
     for c in range(chunks):
-        wide = pl.BlockSpec((4 * LANES, LANES), lambda k: (c * tiles + k, 0))
-        row = pl.BlockSpec((LANES, LANES), lambda k: (c * tiles + k, 0))
-        tail = pl.BlockSpec((8 * tiles, LANES), lambda k: (modes // (8 * tiles) + c, 0))
-        columns = pl.BlockSpec((32, size), lambda k: (0, c))
+        up, down, side, side_left, side_right, low, high = sends[c]
         operands = [f, inner[c], low_in[c], high_in[c], up, down, low, high, low, high]
         operands += [side, side_left, side_right, main, corner]
-        specs = [wide, pair_spec, pair_spec, pair_spec, row, row, row, row, tail, tail, columns, columns, columns]
+        specs = [wide(c), pair, pair, pair, row, row, row, row, tail, tail, columns, columns, columns]
         specs += [
             pl.BlockSpec((5, 8, LANES), lambda k: (0, 0, 0)),
             pl.BlockSpec((16, LANES), lambda k: (0, 0)),
@@ -672,7 +677,7 @@
             out_shape=shape(modes * 4, LANES),
             grid=(tiles,),
             in_specs=specs,
-            out_specs=wide,
+            out_specs=wide(c),
             input_output_aliases=aliases,
             scratch_shapes=[
                 pltpu.VMEM((10, 16, size), f32),

time: 177 us -> 162 us (0.915); the launches traced: 178 us -> 160 us
  waiting for transfers between devices: 30.9 us -> 12.2 us
  local copies, waits for them, and re-layouts: 16.8 us -> 8.78 us
  Pallas kernels: 99 us -> 105 us
  starting transfers between devices: 29.9 us -> 32.6 us
    ppermute x18 -> x22, waiting for transfers between devices: 30.9 us -> 12.2 us  [moved(): lax.ppermute(value, axis, [(i, (i + step) % devices) for i in range(devic...]
    unnamed x26 -> x16, local copies, waits for them, and re-layouts: 16.4 us -> 6.18 us
    pallas_call x7 -> x8, Pallas kernels: 64.5 us -> 69.8 us  [couple(): pl.pallas_call(functools.partial(couple_kernel, cfg), out_shape=shape(2,...]
    ppermute x18 -> x22, starting transfers between devices: 29.9 us -> 32.6 us  [moved(): lax.ppermute(value, axis, [(i, (i + step) % devices) for i in range(devic...]
    pallas_call x3 -> x5, Pallas kernels: 9.64 us -> 8.18 us  [the longest x2 4.41 us: local(): pl.pallas_call(functools.partial(finish_kernel, len(received[c])), out_sh...]
  transfers between devices with their start and end apart: 18 -> 22, of which waited for: 4 -> 4; matrix products, arithmetic and copies ran while one was open for 1% -> 2% of each run, Pallas kernels for 48% -> 59%
where the time goes in v2:
time: 162 us; the launch traced here: 160 us
  Pallas kernels  105 us (65%)
  starting transfers between devices  32.6 us (20%)
  waiting for transfers between devices  12.2 us (8%)
  local copies, waits for them, and re-layouts  8.78 us (5%)
    pallas_call x8, Pallas kernels, couple(): pl.pallas_call(functools.partial(couple_kernel, cfg), out_shape=shape(2,...  69.8 us
    ppermute x22, starting transfers between devices, moved(): lax.ppermute(value, axis, [(i, (i + step) % devices) for i in range(devic...  32.6 us
    pallas_call x2, Pallas kernels, fluxes(): pl.pallas_call(functools.partial(flux_kernel, cfg), out_shape=(halves, ha...  12.6 us
    ppermute x22, waiting for transfers between devices, moved(): lax.ppermute(value, axis, [(i, (i + step) % devices) for i in range(devic...  12.2 us
    pallas_call x2, Pallas kernels, local(): pl.pallas_call(functools.partial(correct_kernel, size), out_shape=shape(m...  12 us
    unnamed x16, local copies, waits for them, and re-layouts  6.18 us
    pallas_call x2, Pallas kernels, local(): pl.pallas_call(functools.partial(finish_kernel, len(received[c])), out_sh...  4.41 us
    pallas_call x1, Pallas kernels, local(): pl.pallas_call(functools.partial(list_kernel, segments, block_mask.shape[...  3.73 us
  transfers between devices with their start and end apart: 22, of which 4 were waited for; matrix products, arithmetic and copies ran while one was open for 2% of the time, Pallas kernels for 59%

profile of v2, /device:TPU:0, one launch (start us, length us, event | category | flops | bytes accessed | tf_op | source)
XLA Modules:
  0.0 160.0 jit_solution(11364749801624078025)
XLA Ops:
  3.6 2.2 %pack.1 = (f32[1040,128]{1,0:T(8,128)}, f32[1040,128]{1,0:T(8,128)}, f32[8,1024]{1,0:T(8,128)S(1)}, f32[8,1024]{1,0:T(8,128)S(1)}) custom-call(f32[4096,128]{1,0:T(8,128)S(1)} %bitcast.17, f32[4,128]{1,0:T(4,128)S(1)} %copy-done.6, f32[32,128]{1,0:T(8,128)S(1)} %bitcast.24), custom_call_target="tpu_custom_call" | custom-call | tf_op jit(solution)/shard_map/pack/pallas_call | solution.py:495
  6.3 2.0 %collective-permute-start.1 = (f32[8,1024]{1,0:T(8,128)S(1)}, f32[8,1024]{1,0:T(8,128)S(1)}, u32[]{:S(2)}, u32[]{:S(2)}) collective-permute-start(f32[8,1024]{1,0:T(8,128)S(1)} %get-tuple-element.52), channel_id=1, source_target_pairs={{0,3},{1,0},{2,1},{3,2},{4,7},{5,4},{6,5},{7,6},{8,11},{9,8},{10,9... | collective-permute-start | bytes 98312 | tf_op jit(solution)/shard_map/ppermute | solution.py:490
  8.2 2.4 %collective-permute-start.4 = (f32[1040,128]{1,0:T(8,128)}, f32[1040,128]{1,0:T(8,128)}, u32[]{:S(2)}, u32[]{:S(2)}) collective-permute-start(f32[1040,128]{1,0:T(8,128)} %get-tuple-element.59), channel_id=1, source_target_pairs={{0,4},{4,8},{8,12},{12,0},{1,5},{5,9},{9,13},{13,1},{2,6},{6,10},{... | collective-permute-start | bytes 1597448 | tf_op jit(solution)/shard_map/ppermute | solution.py:490
  10.6 2.0 %collective-permute-start.5 = (f32[1040,128]{1,0:T(8,128)}, f32[1040,128]{1,0:T(8,128)}, u32[]{:S(2)}, u32[]{:S(2)}) collective-permute-start(f32[1040,128]{1,0:T(8,128)} %get-tuple-element.60), channel_id=1, source_target_pairs={{0,12},{4,0},{8,4},{12,8},{1,13},{5,1},{9,5},{13,9},{2,14},{6,2},{... | collective-permute-start | bytes 1597448 | tf_op jit(solution)/shard_map/ppermute | solution.py:490
  13.5 3.7 %lists.1 = (s32[1120]{0:T(1024)S(1)}, s32[168]{0:T(256)S(1)}, s32[4]{0:T(128)S(1)}) custom-call(s32[2048]{0:T(1024)S(1)} %reshape.26.mask_ref), custom_call_target="tpu_custom_call" | custom-call | tf_op jit(solution)/shard_map/lists/pallas_call | solution.py:513
  18.9 5.7 %flux_inner.1 = (bf16[8320,256]{1,0:T(8,128)(2,1)S(1)}, bf16[8320,256]{1,0:T(8,128)(2,1)S(1)}, f32[2,1024,128]{2,1,0:T(8,128)S(1)}) custom-call(f32[4096,128]{1,0:T(8,128)S(1)} %bitcast.18, f32[8,1024]{1,0:T(8,128)S(1)} %collective-permute-done.refs_1_.refs_3_, f32[8,1024]{1,0:T(8,128)S(1)} %collective-permute-done.1.refs_2_.refs_4_, ...), custom_call_target="tpu_custom_call" | custom-call | flops 1024 | bytes 1024 | tf_op jit(solution)/shard_map/flux_inner/pallas_call | solution.py:530
  24.6 7.8 %couple_other.4 = f32[2,512,128]{2,1,0:T(8,128)S(1)} custom-call(s32[1120]{0:T(1024)S(1)} %get-tuple-element.48.refs_0_, s32[168]{0:T(256)S(1)} %get-tuple-element.49.refs_1_, s32[4]{0:T(128)S(1)} %get-tuple-element.50.refs_2_, f32[8,2048,1024]{2,1,0:T(8,128)} %refs_3_.17, bf16[8320,256]{1,0:T(8,128)(2,1)S(1)} %get-tuple-element.56.refs_4_, ...), custom_call_target="tpu_custom_call" | custom-call | flops 1024 | bytes 1024 | tf_op jit(solution)/shard_map/couple_other/pallas_call | solution.py:553
  32.5 2.8 %collective-permute-start.2 = (f32[2,512,128]{2,1,0:T(8,128)S(1)}, f32[2,512,128]{2,1,0:T(8,128)S(1)}, u32[]{:S(2)}, u32[]{:S(2)}) collective-permute-start(f32[2,512,128]{2,1,0:T(8,128)S(1)} %couple_other.4), channel_id=1, source_target_pairs={{0,16},{16,0},{1,17},{17,1},{2,18},{18,2},{3,19},{19,3},{4,20},{20... | collective-permute-start | bytes 1572872 | tf_op jit(solution)/shard_map/ppermute | solution.py:490
  35.2 8.8 %couple_other.5 = f32[2,512,128]{2,1,0:T(8,128)S(1)} custom-call(s32[1120]{0:T(1024)S(1)} %get-tuple-element.48.refs_0_, s32[168]{0:T(256)S(1)} %get-tuple-element.49.refs_1_, s32[4]{0:T(128)S(1)} %get-tuple-element.50.refs_2_, f32[8,2048,1024]{2,1,0:T(8,128)} %refs_3_.17, bf16[8320,256]{1,0:T(8,128)(2,1)S(1)} %get-tuple-element.56.refs_4_, ...), custom_call_target="tpu_custom_call" | custom-call | flops 1024 | bytes 1024 | tf_op jit(solution)/shard_map/couple_other/pallas_call | solution.py:553
  44.1 9.4 %couple_own.4 = f32[2,512,128]{2,1,0:T(8,128)S(1)} custom-call(s32[1120]{0:T(1024)S(1)} %get-tuple-element.48.refs_0_, s32[168]{0:T(256)S(1)} %get-tuple-element.49.refs_1_, s32[4]{0:T(128)S(1)} %get-tuple-element.50.refs_2_, f32[8,2048,1024]{2,1,0:T(8,128)} %refs_3_.17, bf16[8320,256]{1,0:T(8,128)(2,1)S(1)} %get-tuple-element.56.refs_4_, ...), custom_call_target="tpu_custom_call" | custom-call | flops 1024 | bytes 1024 | tf_op jit(solution)/shard_map/couple_own/pallas_call | solution.py:553
  53.7 8.8 %couple_own.5 = f32[2,512,128]{2,1,0:T(8,128)S(1)} custom-call(s32[1120]{0:T(1024)S(1)} %get-tuple-element.48.refs_0_, s32[168]{0:T(256)S(1)} %get-tuple-element.49.refs_1_, s32[4]{0:T(128)S(1)} %get-tuple-element.50.refs_2_, f32[8,2048,1024]{2,1,0:T(8,128)} %refs_3_.17, bf16[8320,256]{1,0:T(8,128)(2,1)S(1)} %get-tuple-element.56.refs_4_, ...), custom_call_target="tpu_custom_call" | custom-call | flops 1024 | bytes 1024 | tf_op jit(solution)/shard_map/couple_own/pallas_call | solution.py:553
  64.1 1.7 %collective-permute-start.7 = (f32[10,3]{1,0:T(8,128)S(1)}, f32[10,3]{1,0:T(8,128)S(1)}, u32[]{:S(2)}, u32[]{:S(2)}) collective-permute-start(f32[10,3]{1,0:T(8,128)S(1)} %get-tuple-element.97), channel_id=1, source_target_pairs={{0,3},{1,0},{2,1},{3,2},{4,7},{5,4},{6,5},{7,6},{8,11},{9,8},{10,9... | collective-permute-start | bytes 368 | tf_op jit(solution)/shard_map/ppermute | solution.py:490
  65.8 3.8 %collective-permute-start.9 = (f32[2,512,128]{2,1,0:T(8,128)S(1)}, f32[2,512,128]{2,1,0:T(8,128)}, u32[]{:S(2)}, u32[]{:S(2)}) collective-permute-start(f32[2,512,128]{2,1,0:T(8,128)S(1)} %sub.6.inner_ref), channel_id=1, source_target_pairs={{0,12},{4,0},{8,4},{12,8},{1,13},{5,1},{9,5},{13,9},{2,14},{6,2},{... | collective-permute-start | bytes 1572872 | tf_op jit(solution)/shard_map/ppermute | solution.py:490
  70.4 1.6 copy-done.3
  72.0 6.9 %flux_edge.1 = (bf16[8320,256]{1,0:T(8,128)(2,1)S(1)}, bf16[8320,256]{1,0:T(8,128)(2,1)S(1)}, f32[2,1024,128]{2,1,0:T(8,128)S(1)}) custom-call(f32[4096,128]{1,0:T(8,128)S(1)} %bitcast.19, f32[1040,128]{1,0:T(8,128)} %collective-permute-done.4.refs_1_, f32[1040,128]{1,0:T(8,128)} %collective-permute-done.5.refs_2_, ...), custom_call_target="tpu_custom_call" | custom-call | flops 1024 | bytes 1024 | tf_op jit(solution)/shard_map/flux_edge/pallas_call | solution.py:530
  79.0 7.8 %couple_other.6 = f32[2,512,128]{2,1,0:T(8,128)S(1)} custom-call(s32[1120]{0:T(1024)S(1)} %get-tuple-element.48.refs_0_, s32[168]{0:T(256)S(1)} %get-tuple-element.49.refs_1_, s32[4]{0:T(128)S(1)} %get-tuple-element.50.refs_2_, f32[8,2048,1024]{2,1,0:T(8,128)} %refs_3_.17, bf16[8320,256]{1,0:T(8,128)(2,1)S(1)} %get-tuple-element.68.refs_4_, ...), custom_call_target="tpu_custom_call" | custom-call | flops 1024 | bytes 1024 | tf_op jit(solution)/shard_map/couple_other/pallas_call | solution.py:553
  86.8 2.3 %collective-permute-start.10 = (f32[2,512,128]{2,1,0:T(8,128)S(1)}, f32[2,512,128]{2,1,0:T(8,128)S(1)}, u32[]{:S(2)}, u32[]{:S(2)}) collective-permute-start(f32[2,512,128]{2,1,0:T(8,128)S(1)} %couple_other.6), channel_id=1, source_target_pairs={{0,16},{16,0},{1,17},{17,1},{2,18},{18,2},{3,19},{19,3},{4,20},{20... | collective-permute-start | bytes 1572872 | tf_op jit(solution)/shard_map/ppermute | solution.py:490
  89.1 3.8 %collective-permute-start.14 = (f32[2,512,128]{2,1,0:T(8,128)S(1)}, f32[2,512,128]{2,1,0:T(8,128)S(1)}, u32[]{:S(2)}, u32[]{:S(2)}) collective-permute-start(f32[2,512,128]{2,1,0:T(8,128)S(1)} %sub.7.inner_ref), channel_id=1, source_target_pairs={{0,12},{4,0},{8,4},{12,8},{1,13},{5,1},{9,5},{13,9},{2,14},{6,2},{... | collective-permute-start | bytes 1572872 | tf_op jit(solution)/shard_map/ppermute | solution.py:490
  92.9 8.8 %couple_other.7 = f32[2,512,128]{2,1,0:T(8,128)S(1)} custom-call(s32[1120]{0:T(1024)S(1)} %get-tuple-element.48.refs_0_, s32[168]{0:T(256)S(1)} %get-tuple-element.49.refs_1_, s32[4]{0:T(128)S(1)} %get-tuple-element.50.refs_2_, f32[8,2048,1024]{2,1,0:T(8,128)} %refs_3_.17, bf16[8320,256]{1,0:T(8,128)(2,1)S(1)} %get-tuple-element.68.refs_4_, ...), custom_call_target="tpu_custom_call" | custom-call | flops 1024 | bytes 1024 | tf_op jit(solution)/shard_map/couple_other/pallas_call | solution.py:553
  101.9 9.4 %couple_own.6.base_ref = f32[2,512,128]{2,1,0:T(8,128)S(1)} custom-call(s32[1120]{0:T(1024)S(1)} %get-tuple-element.48.refs_0_, s32[168]{0:T(256)S(1)} %get-tuple-element.49.refs_1_, s32[4]{0:T(128)S(1)} %get-tuple-element.50.refs_2_, f32[8,2048,1024]{2,1,0:T(8,128)} %refs_3_.17, bf16[8320,256]{1,0:T(8,128)(2,1)S(1)} %get-tuple-element.68.refs_4_, ...), custom_call_target="tpu_custom_call" | custom-call | flops 1024 | bytes 1024 | tf_op jit(solution)/shard_map/couple_own/pallas_call | solution.py:553
  111.3 2.2 %finish.2 = (f32[544,128]{1,0:T(8,128)S(1)}, f32[544,128]{1,0:T(8,128)S(1)}, f32[4096,128]{1,0:T(8,128)}, f32[32,512]{1,0:T(8,128)S(1)}) custom-call(f32[2,512,128]{2,1,0:T(8,128)S(1)} %sub.6.inner_ref, f32[2,512,128]{2,1,0:T(8,128)S(1)} %couple_own.6.base_ref, f32[2,512,128]{2,1,0:T(8,128)S(1)} %collective-permute-done.10.refs_0_), custom_call_target="tpu_custom_call" | custom-call | flops 1024 | bytes 1024 | tf_op jit(solution)/shard_map/finish/pallas_call | solution.py:644
  113.5 1.7 %collective-permute-start.12 = (f32[32,512]{1,0:T(8,128)S(1)}, f32[32,512]{1,0:T(8,128)S(1)}, u32[]{:S(2)}, u32[]{:S(2)}) collective-permute-start(f32[32,512]{1,0:T(8,128)S(1)} %get-tuple-element.71.side_ref), channel_id=1, source_target_pairs={{0,3},{1,0},{2,1},{3,2},{4,7},{5,4},{6,5},{7,6},{8,11},{9,8},{10,9... | collective-permute-start | bytes 196616 | tf_op jit(solution)/shard_map/ppermute | solution.py:490
  115.3 8.8 %couple_own.7.base_ref = f32[2,512,128]{2,1,0:T(8,128)S(1)} custom-call(s32[1120]{0:T(1024)S(1)} %get-tuple-element.48.refs_0_, s32[168]{0:T(256)S(1)} %get-tuple-element.49.refs_1_, s32[4]{0:T(128)S(1)} %get-tuple-element.50.refs_2_, f32[8,2048,1024]{2,1,0:T(8,128)} %refs_3_.17, bf16[8320,256]{1,0:T(8,128)(2,1)S(1)} %get-tuple-element.68.refs_4_, ...), custom_call_target="tpu_custom_call" | custom-call | flops 1024 | bytes 1024 | tf_op jit(solution)/shard_map/couple_own/pallas_call | solution.py:553
  124.1 2.2 %finish.3 = (f32[544,128]{1,0:T(8,128)S(1)}, f32[544,128]{1,0:T(8,128)S(1)}, f32[4096,128]{1,0:T(8,128)}, f32[32,512]{1,0:T(8,128)S(1)}) custom-call(f32[2,512,128]{2,1,0:T(8,128)S(1)} %sub.7.inner_ref, f32[2,512,128]{2,1,0:T(8,128)S(1)} %couple_own.7.base_ref, f32[2,512,128]{2,1,0:T(8,128)S(1)} %collective-permute-done.15.refs_0_, ...), custom_call_target="tpu_custom_call", output_to_operand_aliasing={{2}: (3, {})} | custom-call | flops 1024 | bytes 1024 | tf_op jit(solution)/shard_map/finish/pallas_call | solution.py:644
  126.4 1.7 %collective-permute-start.17 = (f32[32,512]{1,0:T(8,128)S(1)}, f32[32,512]{1,0:T(8,128)S(1)}, u32[]{:S(2)}, u32[]{:S(2)}) collective-permute-start(f32[32,512]{1,0:T(8,128)S(1)} %get-tuple-element.82.side_ref), channel_id=1, source_target_pairs={{0,3},{1,0},{2,1},{3,2},{4,7},{5,4},{6,5},{7,6},{8,11},{9,8},{10,9... | collective-permute-start | bytes 196616 | tf_op jit(solution)/shard_map/ppermute | solution.py:490
  128.1 3.8 %collective-permute-start.21 = (f32[544,128]{1,0:T(8,128)S(1)}, f32[544,128]{1,0:T(8,128)S(1)}, u32[]{:S(2)}, u32[]{:S(2)}) collective-permute-start(f32[544,128]{1,0:T(8,128)S(1)} %get-tuple-element.92.down_ref), channel_id=1, source_target_pairs={{0,12},{4,0},{8,4},{12,8},{1,13},{5,1},{9,5},{13,9},{2,14},{6,2},{... | collective-permute-start | bytes 835592 | tf_op jit(solution)/shard_map/ppermute | solution.py:490
  132.0 3.8 %collective-permute-start.19 = (f32[544,128]{1,0:T(8,128)S(1)}, f32[544,128]{1,0:T(8,128)S(1)}, u32[]{:S(2)}, u32[]{:S(2)}) collective-permute-start(f32[544,128]{1,0:T(8,128)S(1)} %get-tuple-element.86.down_ref), channel_id=1, source_target_pairs={{0,12},{4,0},{8,4},{12,8},{1,13},{5,1},{9,5},{13,9},{2,14},{6,2},{... | collective-permute-start | bytes 835592 | tf_op jit(solution)/shard_map/ppermute | solution.py:490
  135.8 3.6 %collective-permute-done.20.low_ref.low_x_ref = f32[544,128]{1,0:T(8,128)S(1)} collective-permute-done((f32[544,128]{1,0:T(8,128)S(1)}, f32[544,128]{1,0:T(8,128)S(1)}, u32[]{:S(2)}, u32[]{:S(2)}) %collective-permute-start.20) | collective-permute-done | bytes 278560 | tf_op jit(solution)/shard_map/ppermute | solution.py:490
  139.5 4.5 %collective-permute-done.21.high_ref.high_x_ref = f32[544,128]{1,0:T(8,128)S(1)} collective-permute-done((f32[544,128]{1,0:T(8,128)S(1)}, f32[544,128]{1,0:T(8,128)S(1)}, u32[]{:S(2)}, u32[]{:S(2)}) %collective-permute-start.21) | collective-permute-done | bytes 278560 | tf_op jit(solution)/shard_map/ppermute | solution.py:490
  143.9 6.4 %correct.2.refs_0_ = f32[4096,128]{1,0:T(8,128)} custom-call(f32[4096,128]{1,0:T(8,128)S(1)} %bitcast.20, f32[2,512,128]{2,1,0:T(8,128)S(1)} %sub.6.inner_ref, f32[2,512,128]{2,1,0:T(8,128)} %collective-permute-done.8.low_in_ref, f32[2,512,128]{2,1,0:T(8,128)} %collective-permute-done.9.high_in_ref, f32[544,128]{1,0:T(8,128)S(1)} %get-tuple-element.91.up_ref, ...), custom_call_target="tpu_custom_call" | custom-call | flops 1024 | bytes 1024 | tf_op jit(solution)/shard_map/correct/pallas_call | solution.py:675
  151.4 3.0 %collective-permute-done.19.high_ref.high_x_ref = f32[544,128]{1,0:T(8,128)S(1)} collective-permute-done((f32[544,128]{1,0:T(8,128)S(1)}, f32[544,128]{1,0:T(8,128)S(1)}, u32[]{:S(2)}, u32[]{:S(2)}) %collective-permute-start.19) | collective-permute-done | bytes 278560 | tf_op jit(solution)/shard_map/ppermute | solution.py:490
  154.5 5.6 %correct.3 = f32[4096,128]{1,0:T(8,128)} custom-call(f32[4096,128]{1,0:T(8,128)S(1)} %bitcast.21, f32[2,512,128]{2,1,0:T(8,128)S(1)} %sub.7.inner_ref, f32[2,512,128]{2,1,0:T(8,128)S(1)} %collective-permute-done.13.low_in_ref, f32[2,512,128]{2,1,0:T(8,128)S(1)} %collective-permute-done.14.high_in_ref, ...), custom_call_target="tpu_custom_call", output_to_operand_aliasing={{}: (15, {})} | custom-call | flops 1024 | bytes 1024 | tf_op jit(solution)/shard_map/correct/pallas_call | solution.py:675
  (66 shorter events, 9.8 us)
Async XLA Ops:
  0.6 16.7 %copy-start.7 = (f32[4,128]{1,0:T(4,128)S(1)}, f32[4,128]{1,0:T(4,128)}, u32[]{:S(2)}) copy-start(f32[4,128]{1,0:T(4,128)} %refs_5_.1) | copy-start | bytes 6148
  0.6 1.6 copy-start
  2.2 0.7 copy-start.4
  3.0 0.7 copy-start.6
  3.6 13.7 %copy-start.1 = (f32[1024,4,128]{2,1,0:T(4,128)S(1)}, f32[1024,4,128]{2,1,0:T(4,128)}, u32[]{:S(2)}) copy-start(f32[1024,4,128]{2,1,0:T(4,128)} %param.6) | copy-start | bytes 6291460
  3.6 13.7 %copy-start.5 = (f32[8,4,128]{2,1,0:T(4,128)S(1)}, f32[8,4,128]{2,1,0:T(4,128)}, u32[]{:S(2)}) copy-start(f32[8,4,128]{2,1,0:T(4,128)} %param.9) | copy-start | bytes 49156
  5.8 11.5 %collective-permute-start = (f32[8,1024]{1,0:T(8,128)S(1)}, f32[8,1024]{1,0:T(8,128)S(1)}, u32[]{:S(2)}, u32[]{:S(2)}) collective-permute-start(f32[8,1024]{1,0:T(8,128)S(1)} %get-tuple-element.51), channel_id=1, source_target_pairs={{0,1},{1,2},{2,3},{3,0},{4,5},{5,6},{6,7},{7,4},{8,9},{9,10},{10,1... | collective-permute-start | bytes 98312 | tf_op jit(solution)/shard_map/ppermute | solution.py:490
  6.3 11.0 %collective-permute-start.1 = (f32[8,1024]{1,0:T(8,128)S(1)}, f32[8,1024]{1,0:T(8,128)S(1)}, u32[]{:S(2)}, u32[]{:S(2)}) collective-permute-start(f32[8,1024]{1,0:T(8,128)S(1)} %get-tuple-element.52), channel_id=1, source_target_pairs={{0,3},{1,0},{2,1},{3,2},{4,7},{5,4},{6,5},{7,6},{8,11},{9,8},{10,9... | collective-permute-start | bytes 98312 | tf_op jit(solution)/shard_map/ppermute | solution.py:490
  8.2 54.4 %collective-permute-start.4 = (f32[1040,128]{1,0:T(8,128)}, f32[1040,128]{1,0:T(8,128)}, u32[]{:S(2)}, u32[]{:S(2)}) collective-permute-start(f32[1040,128]{1,0:T(8,128)} %get-tuple-element.59), channel_id=1, source_target_pairs={{0,4},{4,8},{8,12},{12,0},{1,5},{5,9},{9,13},{13,1},{2,6},{6,10},{... | collective-permute-start | bytes 1597448 | tf_op jit(solution)/shard_map/ppermute | solution.py:490
  10.6 52.0 %collective-permute-start.5 = (f32[1040,128]{1,0:T(8,128)}, f32[1040,128]{1,0:T(8,128)}, u32[]{:S(2)}, u32[]{:S(2)}) collective-permute-start(f32[1040,128]{1,0:T(8,128)} %get-tuple-element.60), channel_id=1, source_target_pairs={{0,12},{4,0},{8,4},{12,8},{1,13},{5,1},{9,5},{13,9},{2,14},{6,2},{... | collective-permute-start | bytes 1597448 | tf_op jit(solution)/shard_map/ppermute | solution.py:490
  17.3 1.6 copy-start.2
  32.5 21.1 %collective-permute-start.2 = (f32[2,512,128]{2,1,0:T(8,128)S(1)}, f32[2,512,128]{2,1,0:T(8,128)S(1)}, u32[]{:S(2)}, u32[]{:S(2)}) collective-permute-start(f32[2,512,128]{2,1,0:T(8,128)S(1)} %couple_other.4), channel_id=1, source_target_pairs={{0,16},{16,0},{1,17},{17,1},{2,18},{18,2},{3,19},{19,3},{4,20},{20... | collective-permute-start | bytes 1572872 | tf_op jit(solution)/shard_map/ppermute | solution.py:490
  44.1 18.4 %collective-permute-start.3 = (f32[2,512,128]{2,1,0:T(8,128)S(1)}, f32[2,512,128]{2,1,0:T(8,128)S(1)}, u32[]{:S(2)}, u32[]{:S(2)}) collective-permute-start(f32[2,512,128]{2,1,0:T(8,128)S(1)} %couple_other.5), channel_id=1, source_target_pairs={{0,16},{16,0},{1,17},{17,1},{2,18},{18,2},{3,19},{19,3},{4,20},{20... | collective-permute-start | bytes 1572872 | tf_op jit(solution)/shard_map/ppermute | solution.py:490
  53.6 48.1 %collective-permute-start.8 = (f32[2,512,128]{2,1,0:T(8,128)S(1)}, f32[2,512,128]{2,1,0:T(8,128)}, u32[]{:S(2)}, u32[]{:S(2)}) collective-permute-start(f32[2,512,128]{2,1,0:T(8,128)S(1)} %sub.6.inner_ref), channel_id=1, source_target_pairs={{0,4},{4,8},{8,12},{12,0},{1,5},{5,9},{9,13},{13,1},{2,6},{6,10},{... | collective-permute-start | bytes 1572872 | tf_op jit(solution)/shard_map/ppermute | solution.py:490
  64.0 5.6 %collective-permute-start.6 = (f32[10,3]{1,0:T(8,128)S(1)}, f32[10,3]{1,0:T(8,128)S(1)}, u32[]{:S(2)}, u32[]{:S(2)}) collective-permute-start(f32[10,3]{1,0:T(8,128)S(1)} %get-tuple-element.96), channel_id=1, source_target_pairs={{0,1},{1,2},{2,3},{3,0},{4,5},{5,6},{6,7},{7,4},{8,9},{9,10},{10,1... | collective-permute-start | bytes 368 | tf_op jit(solution)/shard_map/ppermute | solution.py:490
  64.1 5.6 %collective-permute-start.7 = (f32[10,3]{1,0:T(8,128)S(1)}, f32[10,3]{1,0:T(8,128)S(1)}, u32[]{:S(2)}, u32[]{:S(2)}) collective-permute-start(f32[10,3]{1,0:T(8,128)S(1)} %get-tuple-element.97), channel_id=1, source_target_pairs={{0,3},{1,0},{2,1},{3,2},{4,7},{5,4},{6,5},{7,6},{8,11},{9,8},{10,9... | collective-permute-start | bytes 368 | tf_op jit(solution)/shard_map/ppermute | solution.py:490
  65.8 36.1 %collective-permute-start.9 = (f32[2,512,128]{2,1,0:T(8,128)S(1)}, f32[2,512,128]{2,1,0:T(8,128)}, u32[]{:S(2)}, u32[]{:S(2)}) collective-permute-start(f32[2,512,128]{2,1,0:T(8,128)S(1)} %sub.6.inner_ref), channel_id=1, source_target_pairs={{0,12},{4,0},{8,4},{12,8},{1,13},{5,1},{9,5},{13,9},{2,14},{6,2},{... | collective-permute-start | bytes 1572872 | tf_op jit(solution)/shard_map/ppermute | solution.py:490
  70.4 1.6 copy-start.3
  86.8 24.5 %collective-permute-start.10 = (f32[2,512,128]{2,1,0:T(8,128)S(1)}, f32[2,512,128]{2,1,0:T(8,128)S(1)}, u32[]{:S(2)}, u32[]{:S(2)}) collective-permute-start(f32[2,512,128]{2,1,0:T(8,128)S(1)} %couple_other.6), channel_id=1, source_target_pairs={{0,16},{16,0},{1,17},{17,1},{2,18},{18,2},{3,19},{19,3},{4,20},{20... | collective-permute-start | bytes 1572872 | tf_op jit(solution)/shard_map/ppermute | solution.py:490
  89.1 35.0 %collective-permute-start.13 = (f32[2,512,128]{2,1,0:T(8,128)S(1)}, f32[2,512,128]{2,1,0:T(8,128)S(1)}, u32[]{:S(2)}, u32[]{:S(2)}) collective-permute-start(f32[2,512,128]{2,1,0:T(8,128)S(1)} %sub.7.inner_ref), channel_id=1, source_target_pairs={{0,4},{4,8},{8,12},{12,0},{1,5},{5,9},{9,13},{13,1},{2,6},{6,10},{... | collective-permute-start | bytes 1572872 | tf_op jit(solution)/shard_map/ppermute | solution.py:490
  89.1 35.0 %collective-permute-start.14 = (f32[2,512,128]{2,1,0:T(8,128)S(1)}, f32[2,512,128]{2,1,0:T(8,128)S(1)}, u32[]{:S(2)}, u32[]{:S(2)}) collective-permute-start(f32[2,512,128]{2,1,0:T(8,128)S(1)} %sub.7.inner_ref), channel_id=1, source_target_pairs={{0,12},{4,0},{8,4},{12,8},{1,13},{5,1},{9,5},{13,9},{2,14},{6,2},{... | collective-permute-start | bytes 1572872 | tf_op jit(solution)/shard_map/ppermute | solution.py:490
  101.8 22.4 %collective-permute-start.15 = (f32[2,512,128]{2,1,0:T(8,128)S(1)}, f32[2,512,128]{2,1,0:T(8,128)S(1)}, u32[]{:S(2)}, u32[]{:S(2)}) collective-permute-start(f32[2,512,128]{2,1,0:T(8,128)S(1)} %couple_other.7), channel_id=1, source_target_pairs={{0,16},{16,0},{1,17},{17,1},{2,18},{18,2},{3,19},{19,3},{4,20},{20... | collective-permute-start | bytes 1572872 | tf_op jit(solution)/shard_map/ppermute | solution.py:490
  113.5 10.6 %collective-permute-start.11 = (f32[32,512]{1,0:T(8,128)S(1)}, f32[32,512]{1,0:T(8,128)S(1)}, u32[]{:S(2)}, u32[]{:S(2)}) collective-permute-start(f32[32,512]{1,0:T(8,128)S(1)} %get-tuple-element.71.side_ref), channel_id=1, source_target_pairs={{0,1},{1,2},{2,3},{3,0},{4,5},{5,6},{6,7},{7,4},{8,9},{9,10},{10,1... | collective-permute-start | bytes 196616 | tf_op jit(solution)/shard_map/ppermute | solution.py:490
  113.5 10.6 %collective-permute-start.12 = (f32[32,512]{1,0:T(8,128)S(1)}, f32[32,512]{1,0:T(8,128)S(1)}, u32[]{:S(2)}, u32[]{:S(2)}) collective-permute-start(f32[32,512]{1,0:T(8,128)S(1)} %get-tuple-element.71.side_ref), channel_id=1, source_target_pairs={{0,3},{1,0},{2,1},{3,2},{4,7},{5,4},{6,5},{7,6},{8,11},{9,8},{10,9... | collective-permute-start | bytes 196616 | tf_op jit(solution)/shard_map/ppermute | solution.py:490
  126.4 5.6 %collective-permute-start.16 = (f32[32,512]{1,0:T(8,128)S(1)}, f32[32,512]{1,0:T(8,128)S(1)}, u32[]{:S(2)}, u32[]{:S(2)}) collective-permute-start(f32[32,512]{1,0:T(8,128)S(1)} %get-tuple-element.82.side_ref), channel_id=1, source_target_pairs={{0,1},{1,2},{2,3},{3,0},{4,5},{5,6},{6,7},{7,4},{8,9},{9,10},{10,1... | collective-permute-start | bytes 196616 | tf_op jit(solution)/shard_map/ppermute | solution.py:490
  126.4 5.6 %collective-permute-start.17 = (f32[32,512]{1,0:T(8,128)S(1)}, f32[32,512]{1,0:T(8,128)S(1)}, u32[]{:S(2)}, u32[]{:S(2)}) collective-permute-start(f32[32,512]{1,0:T(8,128)S(1)} %get-tuple-element.82.side_ref), channel_id=1, source_target_pairs={{0,3},{1,0},{2,1},{3,2},{4,7},{5,4},{6,5},{7,6},{8,11},{9,8},{10,9... | collective-permute-start | bytes 196616 | tf_op jit(solution)/shard_map/ppermute | solution.py:490
  128.1 11.3 %collective-permute-start.20 = (f32[544,128]{1,0:T(8,128)S(1)}, f32[544,128]{1,0:T(8,128)S(1)}, u32[]{:S(2)}, u32[]{:S(2)}) collective-permute-start(f32[544,128]{1,0:T(8,128)S(1)} %get-tuple-element.91.up_ref), channel_id=1, source_target_pairs={{0,4},{4,8},{8,12},{12,0},{1,5},{5,9},{9,13},{13,1},{2,6},{6,10},{... | collective-permute-start | bytes 835592 | tf_op jit(solution)/shard_map/ppermute | solution.py:490
  128.1 15.8 %collective-permute-start.21 = (f32[544,128]{1,0:T(8,128)S(1)}, f32[544,128]{1,0:T(8,128)S(1)}, u32[]{:S(2)}, u32[]{:S(2)}) collective-permute-start(f32[544,128]{1,0:T(8,128)S(1)} %get-tuple-element.92.down_ref), channel_id=1, source_target_pairs={{0,12},{4,0},{8,4},{12,8},{1,13},{5,1},{9,5},{13,9},{2,14},{6,2},{... | collective-permute-start | bytes 835592 | tf_op jit(solution)/shard_map/ppermute | solution.py:490
  132.0 19.5 %collective-permute-start.18 = (f32[544,128]{1,0:T(8,128)S(1)}, f32[544,128]{1,0:T(8,128)S(1)}, u32[]{:S(2)}, u32[]{:S(2)}) collective-permute-start(f32[544,128]{1,0:T(8,128)S(1)} %get-tuple-element.85.up_ref), channel_id=1, source_target_pairs={{0,4},{4,8},{8,12},{12,0},{1,5},{5,9},{9,13},{13,1},{2,6},{6,10},{... | collective-permute-start | bytes 835592 | tf_op jit(solution)/shard_map/ppermute | solution.py:490
  132.0 22.4 %collective-permute-start.19 = (f32[544,128]{1,0:T(8,128)S(1)}, f32[544,128]{1,0:T(8,128)S(1)}, u32[]{:S(2)}, u32[]{:S(2)}) collective-permute-start(f32[544,128]{1,0:T(8,128)S(1)} %get-tuple-element.86.down_ref), channel_id=1, source_target_pairs={{0,12},{4,0},{8,4},{12,8},{1,13},{5,1},{9,5},{13,9},{2,14},{6,2},{... | collective-permute-start | bytes 835592 | tf_op jit(solution)/shard_map/ppermute | solution.py:490
